TPU v7x, 256 devices: a whole 4x4x8 slice. The times are simulated.
256 devices in a mesh: mem: 8 (over y, core), patch: 32 (over x, z).
Axes of the slice: x: 4, y: 4, z: 8, core: 2. Of those that a mesh axis runs over, the one named last changes fastest.
Arguments:
- mesh_latent: bfloat16 [8, 16384, 512], P('mem', 'patch'), may hold values from -6 to 6
- edge_latent: bfloat16 [32768, 512], P('patch'), may hold values from -6 to 6
- grid_edge_latent: bfloat16 [49152, 512], P('patch'), may hold values from -6 to 6
- edge_inner: bfloat16 [1536, 512], replicated, may hold values from -0.15625 to 0.15625
- edge_outer: bfloat16 [512, 512], replicated, may hold values from -0.25 to 0.25
- node_inner: bfloat16 [1024, 512], replicated, may hold values from -0.1875 to 0.1875
- node_outer: bfloat16 [512, 512], replicated, may hold values from -0.25 to 0.25
- grid_inner: bfloat16 [1024, 512], replicated, may hold values from -0.1875 to 0.1875
- grid_outer: bfloat16 [512, 512], replicated, may hold values from -0.25 to 0.25
- out_weight: bfloat16 [87, 512], replicated, may hold values from -0.25 to 0.25
- prior_state: float32 [87, 16384], P(None, 'patch'), may hold values from -6 to 6
- target: float32 [87, 16384], P(None, 'patch'), may hold values from -6 to 6
- channel_weight: float32 [87], replicated, may hold values from 0.2 to 2
- area_weight: float32 [16384], P('patch'), may hold values from 0.2 to 2
- send_rows: int32 [32, 2, 96], P('patch'), may hold values from 0 to 511
- edge_senders: int32 [32768], P('patch'), may hold values from 0 to 703, as said below
- edge_receivers: int32 [32768], P('patch'), may hold values from 0 to 511
- edge_count: int32 [32], P('patch'), may hold values from 256 to 1024, as said below
- grid_senders: int32 [49152], P('patch'), may hold values from 0 to 703, as said below
Outputs:
- crps_gradient: float32 [8, 87, 16384], P('mem', None, 'patch')
Inputs may be any that keep to these rules, and one draw needn't show every extreme that they name: `edge_senders`: values below 512 name a row of the band itself, values from 512 to 607 a row received from the previous band, larger values a row received from the next band; the first band names none of the second kind and the last band none of the third. `grid_senders`: as for edge_senders: own rows, rows from the previous band, rows from the next band; the first and last bands name only bands that exist. The live slots of a band are its first edge_count slots; some band has all 1024 slots live.
All inputs are finite; a program needn't handle non-finite values.
Results may differ from a plain program's by a relative error of at most 0.023.
Values may be sent and summed in bfloat16 or wider, within the bound.
A program may use at most 64 MiB of HBM per device.

v0:
```python
import jax
import jax.numpy as jnp
from jax import lax
from jax.sharding import PartitionSpec as P

epsilon = 1e-05
smooth = 0.25


def shifted(block, axis, distance):
    devices = range(lax.axis_size(axis))
    route = [(i - distance, i) for i in devices if i - distance in devices]
    return lax.ppermute(block, axis, route)


def layer_norm(values):
    average = jnp.mean(values, -1, keepdims=True)
    centred = values - average
    spread = jnp.mean(centred * centred, -1, keepdims=True)
    return centred / jnp.sqrt(spread + epsilon)


def network(inputs, inner_weight, outer_weight):
    inner = jax.nn.silu(jnp.dot(inputs, inner_weight, preferred_element_type=jnp.float32)).astype(
        jnp.bfloat16
    )
    return layer_norm(jnp.dot(inner, outer_weight, preferred_element_type=jnp.float32))


def smooth_slope(values):
    return values / jnp.sqrt(values * values + smooth * smooth)


def selector(rows, length):
    return (rows[:, None] == jnp.arange(length, dtype=jnp.int32)[None, :]).astype(jnp.bfloat16)


def pick_rows(table, rows):
    return jnp.dot(
        selector(rows, table.shape[0]), table, preferred_element_type=jnp.float32
    ).astype(jnp.bfloat16)


def add_into(message, receivers, nodes):
    placing = (jnp.arange(nodes, dtype=jnp.int32)[:, None] == receivers[None, :]).astype(
        jnp.float32
    )
    return jnp.dot(
        placing, message, preferred_element_type=jnp.float32, precision=lax.Precision.HIGHEST
    )


def extend(latent, sends):
    lower = shifted(pick_rows(latent, sends[0]), "patch", 1)
    upper = shifted(pick_rows(latent, sends[1]), "patch", -1)
    return jnp.concatenate([latent, lower, upper], 0)


def per_device(
    mesh_latent,
    edge_latent,
    grid_edge_latent,
    edge_inner,
    edge_outer,
    node_inner,
    node_outer,
    grid_inner,
    grid_outer,
    out_weight,
    prior_state,
    target,
    channel_weight,
    area_weight,
    send_rows,
    edge_senders,
    edge_receivers,
    edge_count,
    grid_senders,
):
    latent = mesh_latent[0]
    sends = send_rows[0]
    live_count = edge_count[0]
    nodes = latent.shape[0]
    edges = edge_senders.shape[0]
    width = latent.shape[1]
    extended = extend(latent, sends)
    inputs = jnp.concatenate(
        [pick_rows(extended, edge_senders), pick_rows(latent, edge_receivers), edge_latent], 1
    )
    message = network(inputs, edge_inner, edge_outer)
    live_slots = jnp.arange(edges, dtype=jnp.int32) < live_count
    message = jnp.where(live_slots[:, None], message, 0.0)
    summed = add_into(message, edge_receivers, nodes)
    node_inputs = jnp.concatenate([latent, summed.astype(jnp.bfloat16)], 1)
    updated = (latent.astype(jnp.float32) + network(node_inputs, node_inner, node_outer)).astype(
        jnp.bfloat16
    )
    extended_new = extend(updated, sends)
    grid_inputs = jnp.concatenate([pick_rows(extended_new, grid_senders), grid_edge_latent], 1)
    grid_message = network(grid_inputs, grid_inner, grid_outer)
    grid_sum = grid_message.reshape(-1, 3, width).sum(1).astype(jnp.bfloat16)
    output = lax.dot_general(
        out_weight, grid_sum, (((1,), (1,)), ((), ())), preferred_element_type=jnp.float32
    )
    difference = prior_state + output - target
    everyone = lax.all_gather(
        difference[None].astype(jnp.bfloat16), "mem", axis=0, tiled=True
    ).astype(jnp.float32)
    pairwise = jnp.sum(smooth_slope(difference[None] - everyone), 0)
    result = smooth_slope(difference) - pairwise / (everyone.shape[0] - 1)
    gradient = result * channel_weight[:, None] * area_weight[None, :]
    return gradient[None]


def solution(mesh):
    in_specs = (
        P("mem", "patch", None),
        P("patch", None),
        P("patch", None),
        P(),
        P(),
        P(),
        P(),
        P(),
        P(),
        P(),
        P(None, "patch"),
        P(None, "patch"),
        P(),
        P("patch"),
        P("patch", None, None),
        P("patch"),
        P("patch"),
        P("patch"),
        P("patch"),
    )
    out_specs = P("mem", None, "patch")
    return jax.shard_map(
        per_device, mesh=mesh, in_specs=in_specs, out_specs=out_specs, check_vma=False
    )
```

profile of v0, /device:TPU:7, one launch (start us, length us, event | category | flops | bytes accessed | tf_op | source)
XLA Modules:
  0.0 92.8 jit_solution(3815639665118770481)
XLA Ops:
  0.0 0.0 copy-start
  0.0 0.8 slice_bitcast_fusion.1
  0.8 1.4 %convolution_convert_fusion.2 = bf16[96,512]{1,0:T(8,128)(2,1)S(1)} fusion(bf16[1,512,512]{2,1,0:T(8,128)(2,1)} %param.19, s32[96]{0:T(128)S(1)} %get-tuple-element.6), kind=kOutput, calls=%fused_computation.44 | convolution fusion | flops 50429952 | bytes 622976 | tf_op jit(solution)/shard_map/dot_general | solution.py:39
  2.2 7.8 %collective-permute-start.1 = (bf16[96,512]{1,0:T(8,128)(2,1)S(1)}, bf16[96,512]{1,0:T(8,128)(2,1)S(1)}, u32[]{:S(2)}, u32[]{:S(2)}) collective-permute-start(bf16[96,512]{1,0:T(8,128)(2,1)S(1)} %convolution_convert_fusion.2), channel_id=1, source_target_pairs={{1,0},{2,1},{3,2},{4,3},{5,4},{6,5},{7,6},{8,7},{9,8},{10,9},{11,1... | collective-permute-start | bytes 294920 | tf_op jit(solution)/shard_map/ppermute | solution.py:13
  9.9 1.3 %convolution_convert_fusion.3 = bf16[96,512]{1,0:T(8,128)(2,1)S(1)} fusion(bf16[1,512,512]{2,1,0:T(8,128)(2,1)} %param.19, s32[96]{0:T(128)S(1)} %get-tuple-element.5), kind=kOutput, calls=%fused_computation.45 | convolution fusion | flops 50429952 | bytes 622976 | tf_op jit(solution)/shard_map/dot_general | solution.py:39
  11.2 1.9 %collective-permute-start = (bf16[96,512]{1,0:T(8,128)(2,1)S(1)}, bf16[96,512]{1,0:T(8,128)(2,1)S(1)}, u32[]{:S(2)}, u32[]{:S(2)}) collective-permute-start(bf16[96,512]{1,0:T(8,128)(2,1)S(1)} %convolution_convert_fusion.3), channel_id=1, source_target_pairs={{0,1},{1,2},{2,3},{3,4},{4,5},{5,6},{6,7},{7,8},{8,9},{9,10},{10,1... | collective-permute-start | bytes 294920 | tf_op jit(solution)/shard_map/ppermute | solution.py:13
  13.2 1.3 %copy.31 = bf16[1,512,512]{1,2,0:T(8,128)(2,1)S(1)} copy(bf16[1,512,512]{2,1,0:T(8,128)(2,1)} %param.19) | data formatting | bytes 1048576 | tf_op args[0]
  15.1 2.3 %copy.34 = bf16[1024,512]{0,1:T(8,128)(2,1)} copy(bf16[1024,512]{1,0:T(8,128)(2,1)} %param.20) | data formatting | bytes 2097152 | tf_op args[1]
  17.4 1.9 %fusion.22 = bf16[1024,512]{0,1:T(8,128)(2,1)} fusion(s32[1024]{0:T(1024)S(1)} %copy-done.15, bf16[1,512,512]{2,1,0:T(8,128)(2,1)S(1)} %copy-done.2), kind=kOutput, calls=%fused_computation.29 | convolution fusion | flops 537919488 | bytes 1576960 | tf_op jit(solution)/shard_map/dot_general | solution.py:39
  19.3 0.0 collective-permute-done.1
  19.3 0.1 copy.33
  19.4 0.0 collective-permute-done
  19.4 0.1 copy.32
  19.6 0.0 copy-start.11
  19.6 2.1 %fusion.23 = bf16[1024,512]{0,1:T(8,128)(2,1)} fusion(s32[1024]{0:T(1024)S(1)} %copy-done.14, bf16[96,512]{0,1:T(8,128)(2,1)S(1)} %copy.33, bf16[96,512]{0,1:T(8,128)(2,1)S(1)} %copy.32, bf16[512,512]{0,1:T(8,128)(2,1)S(1)} %bitcast.37), kind=kOutput, calls=%fused_computation.30 | convolution fusion | flops 741605376 | bytes 1773568 | tf_op jit(solution)/shard_map/dot_general | solution.py:39
  21.7 5.8 %fusion.88 = (f32[1024]{0:T(1024)S(1)}, f32[1024,512]{0,1:T(8,128)}) fusion(bf16[512,512]{1,0:T(8,128)(2,1)S(1)} %copy-done.11, bf16[1536,512]{1,0:T(8,128)(2,1)S(1)} %copy-done, bf16[1024,512]{0,1:T(8,128)(2,1)} %copy.34, bf16[1024,512]{0,1:T(8,128)(2,1)} %fusion.22, bf16[1024,512]{0,1:T(8,128)(2,1)} %fusion.23), kind=kOutput, calls=%fused_computation.102 | convolution fusion | flops 2160065536 | bytes 7344128 | tf_op jit(solution)/shard_map/dot_general | solution.py:27
  27.6 2.0 %multiply_reduce_fusion.1 = f32[1024]{0:T(1024)S(1)} fusion(f32[1024,512]{0,1:T(8,128)} %get-tuple-element.8, f32[1024]{0:T(1024)S(1)} %broadcast_multiply_fusion.1), kind=kLoop, calls=%fused_computation.22 | loop fusion | flops 1571840 | bytes 2105344 | tf_op jit(solution)/shard_map/reduce_sum | solution.py:19
  29.5 0.2 copy-done.3
  29.8 3.0 %fusion.32 = bf16[512,512]{0,1:T(8,128)(2,1)} fusion(f32[1024,512]{0,1:T(8,128)S(1)} %copy-done.3, f32[1024]{0:T(1024)S(1)} %add_sqrt_fusion.1, f32[1024]{0:T(1024)S(1)} %broadcast_multiply_fusion.1, s32[1024]{0:T(1024)S(1)} %copy-done.15, pred[1024]{0:T(1024)(128)(4,1)S(1)} %iota_compare_fusion.22), kind=kOutput, calls=%fused_computation.38 | convolution fusion | flops 3223584768 | bytes 2634752 | tf_op jit(solution)/shard_map/dot_general | solution.py:48
  32.7 3.5 %fusion.91 = (f32[512]{0:T(512)S(1)}, f32[512,512]{1,0:T(8,128)}) fusion(bf16[512,512]{1,0:T(8,128)(2,1)S(1)} %copy-done.12, bf16[1024,512]{1,0:T(8,128)(2,1)} %param.24, bf16[512,512]{0,1:T(8,128)(2,1)} %fusion.32, bf16[512,512]{0,1:T(8,128)(2,1)S(1)} %bitcast.38), kind=kOutput, calls=%fused_computation.103 | convolution fusion | flops 808975872 | bytes 3672064 | tf_op jit(solution)/shard_map/dot_general | solution.py:27
  36.3 1.6 %copy.35 = f32[512,512]{0,1:T(8,128)S(1)} copy(f32[512,512]{1,0:T(8,128)} %get-tuple-element.10) | data formatting | bytes 2097152 | tf_op jit(solution)/shard_map/dot_general | solution.py:27
  37.8 0.2 multiply_reduce_fusion.2
  38.0 1.2 %add_convert_fusion = bf16[512,512]{0,1:T(8,128)(2,1)S(1)} fusion(f32[512,512]{0,1:T(8,128)S(1)} %copy.35, f32[512]{0:T(512)S(1)} %add_sqrt_fusion.2, f32[512]{0:T(512)S(1)} %broadcast_multiply_fusion.2, bf16[1,512,512]{1,2,0:T(8,128)(2,1)} %copy-done.4), kind=kLoop, calls=%fused_computation.50 | loop fusion | flops 1310720 | bytes 2101248 | tf_op jit(solution)/shard_map/convert_element_type | solution.py:95
  39.3 0.3 convolution_convert_fusion.1
  39.6 0.0 copy-start.13
  39.6 2.1 %collective-permute-start.2 = (bf16[96,512]{1,0:T(8,128)(2,1)S(1)}, bf16[96,512]{1,0:T(8,128)(2,1)S(1)}, u32[]{:S(2)}, u32[]{:S(2)}) collective-permute-start(bf16[96,512]{1,0:T(8,128)(2,1)S(1)} %convolution_convert_fusion.1), channel_id=1, source_target_pairs={{0,1},{1,2},{2,3},{3,4},{4,5},{5,6},{6,7},{7,8},{8,9},{9,10},{10,1... | collective-permute-start | bytes 294920 | tf_op jit(solution)/shard_map/ppermute | solution.py:13
  41.6 0.3 convolution_convert_fusion
  41.9 5.7 %collective-permute-start.3 = (bf16[96,512]{1,0:T(8,128)(2,1)S(1)}, bf16[96,512]{1,0:T(8,128)(2,1)S(1)}, u32[]{:S(2)}, u32[]{:S(2)}) collective-permute-start(bf16[96,512]{1,0:T(8,128)(2,1)S(1)} %convolution_convert_fusion), channel_id=1, source_target_pairs={{1,0},{2,1},{3,2},{4,3},{5,4},{6,5},{7,6},{8,7},{9,8},{10,9},{11,1... | collective-permute-start | bytes 294920 | tf_op jit(solution)/shard_map/ppermute | solution.py:13
  47.6 2.6 %copy.38 = bf16[1536,512]{0,1:T(8,128)(2,1)} copy(bf16[1536,512]{1,0:T(8,128)(2,1)} %param.21) | data formatting | bytes 3145728 | tf_op args[2]
  50.2 0.0 collective-permute-done.2
  50.2 0.1 copy.36
  50.3 0.0 collective-permute-done.3
  50.3 0.1 copy.37
  50.4 0.0 copy-start.10
  50.4 2.7 %fusion.12 = bf16[1536,512]{0,1:T(8,128)(2,1)} fusion(s32[1536]{0:T(1024)S(1)} %copy-done.13, bf16[96,512]{0,1:T(8,128)(2,1)S(1)} %copy.37, bf16[96,512]{0,1:T(8,128)(2,1)S(1)} %copy.36, bf16[512,512]{0,1:T(8,128)(2,1)S(1)} %add_convert_fusion), kind=kOutput, calls=%fused_computation.16 | convolution fusion | flops 1111326720 | bytes 2299904 | tf_op jit(solution)/shard_map/dot_general | solution.py:39
  53.2 6.6 %fusion.94 = (f32[1536]{0:T(1024)S(1)}, f32[1536,512]{1,0:T(8,128)}) fusion(bf16[512,512]{1,0:T(8,128)(2,1)} %param.27, bf16[1024,512]{1,0:T(8,128)(2,1)S(1)} %copy-done.10, bf16[1536,512]{0,1:T(8,128)(2,1)} %copy.38, bf16[1536,512]{0,1:T(8,128)(2,1)} %fusion.12), kind=kOutput, calls=%fused_computation.104 | convolution fusion | flops 2426927616 | bytes 7870464 | tf_op jit(solution)/shard_map/dot_general | solution.py:27
  59.8 2.6 %multiply_reduce_fusion = f32[1536]{0:T(1024)S(1)} fusion(f32[1536,512]{1,0:T(8,128)} %get-tuple-element.12, f32[1536]{0:T(1024)S(1)} %broadcast_multiply_fusion), kind=kLoop, calls=%fused_computation.12 | loop fusion | flops 2357760 | bytes 3158016 | tf_op jit(solution)/shard_map/reduce_sum | solution.py:19
  62.4 0.2 copy-done.1
  62.7 2.2 %subtract_divide_fusion = f32[1536,512]{1,0:T(8,128)} fusion(f32[1536,512]{1,0:T(8,128)S(1)} %copy-done.1, f32[1536]{0:T(1024)S(1)} %add_sqrt_fusion, f32[1536]{0:T(1024)S(1)} %broadcast_multiply_fusion), kind=kLoop, calls=%fused_computation.17 | loop fusion | flops 1572864 | bytes 6303744 | tf_op jit(solution)/shard_map/div | solution.py:20
  64.8 5.8 %reshape.57 = f32[512,3,512]{2,1,0:T(4,128)} reshape(f32[1536,512]{1,0:T(8,128)} %subtract_divide_fusion) | data formatting | bytes 6291456 | tf_op jit(solution)/shard_map/reshape | solution.py:101
  70.6 4.8 %reduce_sum.78 = bf16[512,512]{1,0:T(8,128)(2,1)S(1)} reduce(f32[512,3,512]{2,1,0:T(4,128)} %reshape.57, f32[]{:T(128)} %constant.12.clone.1), dimensions={1}, to_apply=%region_6.7 | reduce | flops 524288 | bytes 3670020 | tf_op jit(solution)/shard_map/reduce_sum | solution.py:101
  75.5 0.0 copy-start.8
  75.5 0.0 copy-start.9
  75.5 0.3 fusion.36
  75.8 15.6 %all-gather.1 = bf16[8,87,512]{2,1,0:T(8,128)(2,1)S(1)} all-gather(bf16[1,87,512]{2,1,0:T(8,128)(2,1)S(1)} %convert_bitcast_fusion), channel_id=2, replica_groups=mesh['mem'=8,'patch'=32] {'mem'}, dimensions={0}, use_global_device_ids=true | all-gather | bytes 801792 | tf_op jit(solution)/shard_map/all_gather | solution.py:106
  91.5 0.3 fusion.31
  91.8 0.1 multiply_bitcast_fusion
  91.9 0.9 copy.39
  (32 shorter events, 0.1 us)
Async XLA Ops:
  0.0 21.7 %copy-start = (bf16[1536,512]{1,0:T(8,128)(2,1)S(1)}, bf16[1536,512]{1,0:T(8,128)(2,1)}, u32[]{:S(2)}) copy-start(bf16[1536,512]{1,0:T(8,128)(2,1)} %param.22) | copy-start | bytes 4718596
  0.8 16.6 %copy-start.2 = (bf16[1,512,512]{2,1,0:T(8,128)(2,1)S(1)}, bf16[1,512,512]{2,1,0:T(8,128)(2,1)}, u32[]{:S(2)}) copy-start(bf16[1,512,512]{2,1,0:T(8,128)(2,1)} %param.19) | copy-start | bytes 1572868
  0.8 16.6 %copy-start.15 = (s32[1024]{0:T(1024)S(1)}, s32[1024]{0:T(1024)}, u32[]{:S(2)}) copy-start(s32[1024]{0:T(1024)} %param.35) | copy-start | bytes 12292
  2.2 17.1 %collective-permute-start.1 = (bf16[96,512]{1,0:T(8,128)(2,1)S(1)}, bf16[96,512]{1,0:T(8,128)(2,1)S(1)}, u32[]{:S(2)}, u32[]{:S(2)}) collective-permute-start(bf16[96,512]{1,0:T(8,128)(2,1)S(1)} %convolution_convert_fusion.2), channel_id=1, source_target_pairs={{1,0},{2,1},{3,2},{4,3},{5,4},{6,5},{7,6},{8,7},{9,8},{10,9},{11,1... | collective-permute-start | bytes 294920 | tf_op jit(solution)/shard_map/ppermute | solution.py:13
  11.2 8.2 %collective-permute-start = (bf16[96,512]{1,0:T(8,128)(2,1)S(1)}, bf16[96,512]{1,0:T(8,128)(2,1)S(1)}, u32[]{:S(2)}, u32[]{:S(2)}) collective-permute-start(bf16[96,512]{1,0:T(8,128)(2,1)S(1)} %convolution_convert_fusion.3), channel_id=1, source_target_pairs={{0,1},{1,2},{2,3},{3,4},{4,5},{5,6},{6,7},{7,8},{8,9},{9,10},{10,1... | collective-permute-start | bytes 294920 | tf_op jit(solution)/shard_map/ppermute | solution.py:13
  14.4 18.3 %copy-start.4 = (bf16[1,512,512]{1,2,0:T(8,128)(2,1)}, bf16[1,512,512]{1,2,0:T(8,128)(2,1)S(1)}, u32[]{:S(2)}) copy-start(bf16[1,512,512]{1,2,0:T(8,128)(2,1)S(1)} %copy.31) | copy-start | bytes 1572868
  17.4 2.2 %copy-start.14 = (s32[1024]{0:T(1024)S(1)}, s32[1024]{0:T(1024)}, u32[]{:S(2)}) copy-start(s32[1024]{0:T(1024)} %param.34) | copy-start | bytes 12292
  19.6 2.1 %copy-start.11 = (bf16[512,512]{1,0:T(8,128)(2,1)S(1)}, bf16[512,512]{1,0:T(8,128)(2,1)}, u32[]{:S(2)}) copy-start(bf16[512,512]{1,0:T(8,128)(2,1)} %param.23) | copy-start | bytes 1572868
  27.5 2.2 %copy-start.3 = (f32[1024,512]{0,1:T(8,128)S(1)}, f32[1024,512]{0,1:T(8,128)}, u32[]{:S(2)}) copy-start(f32[1024,512]{0,1:T(8,128)} %get-tuple-element.8) | copy-start | bytes 6291460
  29.8 3.0 %copy-start.12 = (bf16[512,512]{1,0:T(8,128)(2,1)S(1)}, bf16[512,512]{1,0:T(8,128)(2,1)}, u32[]{:S(2)}) copy-start(bf16[512,512]{1,0:T(8,128)(2,1)} %param.25) | copy-start | bytes 1572868
  39.6 10.9 %copy-start.13 = (s32[1536]{0:T(1024)S(1)}, s32[1536]{0:T(1024)}, u32[]{:S(2)}) copy-start(s32[1536]{0:T(1024)} %param.37) | copy-start | bytes 18436
  39.6 10.6 %collective-permute-start.2 = (bf16[96,512]{1,0:T(8,128)(2,1)S(1)}, bf16[96,512]{1,0:T(8,128)(2,1)S(1)}, u32[]{:S(2)}, u32[]{:S(2)}) collective-permute-start(bf16[96,512]{1,0:T(8,128)(2,1)S(1)} %convolution_convert_fusion.1), channel_id=1, source_target_pairs={{0,1},{1,2},{2,3},{3,4},{4,5},{5,6},{6,7},{7,8},{8,9},{9,10},{10,1... | collective-permute-start | bytes 294920 | tf_op jit(solution)/shard_map/ppermute | solution.py:13
  41.9 8.4 %collective-permute-start.3 = (bf16[96,512]{1,0:T(8,128)(2,1)S(1)}, bf16[96,512]{1,0:T(8,128)(2,1)S(1)}, u32[]{:S(2)}, u32[]{:S(2)}) collective-permute-start(bf16[96,512]{1,0:T(8,128)(2,1)S(1)} %convolution_convert_fusion), channel_id=1, source_target_pairs={{1,0},{2,1},{3,2},{4,3},{5,4},{6,5},{7,6},{8,7},{9,8},{10,9},{11,1... | collective-permute-start | bytes 294920 | tf_op jit(solution)/shard_map/ppermute | solution.py:13
  50.4 2.8 %copy-start.10 = (bf16[1024,512]{1,0:T(8,128)(2,1)S(1)}, bf16[1024,512]{1,0:T(8,128)(2,1)}, u32[]{:S(2)}) copy-start(bf16[1024,512]{1,0:T(8,128)(2,1)} %param.26) | copy-start | bytes 3145732
  59.8 2.8 %copy-start.1 = (f32[1536,512]{1,0:T(8,128)S(1)}, f32[1536,512]{1,0:T(8,128)}, u32[]{:S(2)}) copy-start(f32[1536,512]{1,0:T(8,128)} %get-tuple-element.12) | copy-start | bytes 9437188
  70.6 4.8 %copy-start.5 = (f32[87,512]{1,0:T(8,128)S(1)}, f32[87,512]{1,0:T(8,128)}, u32[]{:S(2)}) copy-start(f32[87,512]{1,0:T(8,128)} %param.30) | copy-start | bytes 534532
  70.6 4.9 %copy-start.6 = (f32[87,512]{1,0:T(8,128)S(1)}, f32[87,512]{1,0:T(8,128)}, u32[]{:S(2)}) copy-start(f32[87,512]{1,0:T(8,128)} %param.29) | copy-start | bytes 534532
  70.6 4.9 %copy-start.7 = (bf16[87,512]{1,0:T(8,128)(2,1)S(1)}, bf16[87,512]{1,0:T(8,128)(2,1)}, u32[]{:S(2)}) copy-start(bf16[87,512]{1,0:T(8,128)(2,1)} %param.28) | copy-start | bytes 267268
  75.5 16.3 %copy-start.8 = (f32[512]{0:T(512)S(1)}, f32[512]{0:T(512)}, u32[]{:S(2)}) copy-start(f32[512]{0:T(512)} %param.32) | copy-start | bytes 6148
  75.5 16.3 %copy-start.9 = (f32[87]{0:T(128)S(1)}, f32[87]{0:T(128)}, u32[]{:S(2)}) copy-start(f32[87]{0:T(128)} %param.31) | copy-start | bytes 1048
where the time goes:
time: 93.4 us; the launch traced here: 92.8 us
  matrix products  29.3 us (31%)
  starting transfers between devices  17.4 us (19%)
  local copies, waits for them, and re-layouts  16.1 us (17%)
  blocking collectives  15.6 us (17%)
  other arithmetic  13.4 us (14%)
    ppermute x4, starting transfers between devices, shifted(): return lax.ppermute(block, axis, route)  17.4 us
    dot_general x3, matrix products, network(): jnp.dot(inner, outer_weight, preferred_element_type=jnp.float32)  16 us
    all_gather x1, blocking collectives, per_device(): lax.all_gather(difference[None].astype(jnp.bfloat16), 'mem', axis=0, tile...  15.6 us
    dot_general x7, matrix products, pick_rows(): jnp.dot(selector(rows, table.shape[0]), table, preferred_element_type=jnp...  10 us
    unnamed x35, local copies, waits for them, and re-layouts  6.64 us
    reshape x1, local copies, waits for them, and re-layouts, per_device(): grid_sum = grid_message.reshape(-1, 3, width).sum(1).astype(jnp.bfloat16)  5.81 us
    reduce_sum x1, other arithmetic, per_device(): grid_sum = grid_message.reshape(-1, 3, width).sum(1).astype(jnp.bfloat16)  4.83 us
    reduce_sum x3, other arithmetic, layer_norm(): spread = jnp.mean(centred * centred, -1, keepdims=True)  4.75 us
  transfers between devices with their start and end apart: 4, of which 0 were waited for; matrix products, arithmetic and copies ran while one was open for 11% of the time, Pallas kernels for 0%

commit v1 on v0

v1 whole, which is shorter than its diff:
```python
import functools

import jax
import jax.numpy as jnp
from jax import lax
from jax.experimental import pallas as pl
from jax.experimental.pallas import tpu as pltpu
from jax.sharding import PartitionSpec as P

epsilon = 1e-05
smooth = 0.25
f32, bf16 = jnp.float32, jnp.bfloat16
MESH = pl.DeviceIdType.MESH

LANES = 128
WIDTH = 512
NODES = 512
EDGES = 1024
DECODER = 1536
HALO = 96
SENT = 2 * HALO
TABLE = 256
POINTS = 512
CHANNELS = 87
PADDED = 96
HALF = 48
MEMBERS = 8
EDGE_TILE = 256
GRID_TILE = 384
NODE_TILE = 256


def dot(a, b):
    return jnp.dot(a, b, preferred_element_type=f32)


def spread(row):
    return jnp.broadcast_to(row, (LANES, LANES)).T


def one_hot(rows, base, blocks):
    lanes = lax.broadcasted_iota(jnp.int32, rows.shape, 1)
    parts = [
        jnp.where(rows == lanes + (base + LANES * b), 1.0, 0.0).astype(bf16)
        for b in range(blocks)
    ]
    return parts[0] if blocks == 1 else jnp.concatenate(parts, 1)


def silu(v):
    half = 0.5 * v
    return (half + half * jnp.tanh(half)).astype(bf16)


def inverse_spread(centred):
    return lax.rsqrt(jnp.mean(centred * centred, -1, keepdims=True) + epsilon)


def centre(weight):
    wide = weight.astype(f32)
    return (wide - jnp.mean(wide, -1, keepdims=True)).astype(bf16)


def slope(v):
    return v * lax.rsqrt(v * v + smooth * smooth)


def kernel(
    lat_h, elat_h, glat_h, ei_h, eo_h, ni_h, no_h, gi_h, go_h, ow_h, prior_h, target_h,
    cw_h, aw_h, sends_h, es_h, er_h, gs_h, count_s,
    out_ref,
    lat, elat, glat, ws, wr, wp, eo, ni, no, gws, gwp, go, ow, prior, target, cw, aw, sends, es, er, gs,
    chosen, halo, chosen_new, halo_new, table, acc, acc_grid, live, message, updated, readout,
    diff, outgoing, incoming, pairs, answers,
    load_sem, send_sem, recv_sem, send_new_sem, recv_new_sem, out_sem, in_sem, back_sem, answer_sem,
):
    member = lax.axis_index("mem")
    band = lax.axis_index("patch")
    bands = lax.axis_size("patch")
    above = lax.rem(band + 1, bands)
    below = lax.rem(band + bands - 1, bands)

    loads = {}

    def load(name, source, target_ref):
        copy = pltpu.make_async_copy(source, target_ref, load_sem.at[len(loads)])
        copy.start()
        loads[name] = copy

    def ready(*names):
        for name in names:
            loads[name].wait()

    load("sends", sends_h.at[0], sends)
    load("lat", lat_h.at[0], lat)
    load("ws", ei_h.at[pl.ds(0, WIDTH)], ws)
    load("wr", ei_h.at[pl.ds(WIDTH, WIDTH)], wr)
    load("es", es_h, es)
    load("er", er_h, er)
    load("we", ei_h.at[pl.ds(2 * WIDTH, WIDTH)], wp.at[pl.ds(0, WIDTH)])
    load("elat", elat_h, elat)
    load("eo", eo_h, eo)
    load("ni", ni_h, ni)
    load("no", no_h, no)
    load("gws", gi_h.at[pl.ds(0, WIDTH)], gws)
    load("gwe", gi_h.at[pl.ds(WIDTH, WIDTH)], gwp.at[pl.ds(0, WIDTH)])
    load("gs", gs_h, gs)
    load("glat", glat_h, glat)
    load("go", go_h, go)
    load("ow", ow_h, ow)
    load("prior", prior_h, prior)
    load("target", target_h, target)
    load("cw", cw_h, cw)
    load("aw", aw_h, aw)

    barrier = pltpu.get_barrier_semaphore()
    for neighbour in (above, below):
        pl.semaphore_signal(barrier, inc=1, device_id=(member, neighbour), device_id_type=MESH)
    for k in range(1, MEMBERS):
        peer = lax.rem(member + k, MEMBERS)
        pl.semaphore_signal(barrier, inc=1, device_id=(peer, band), device_id_type=MESH)

    ready("sends")
    up = spread(jnp.concatenate([sends[0:1, :], jnp.zeros((1, LANES - HALO), jnp.int32)], 1))
    down = spread(jnp.concatenate([sends[1:2, :], jnp.zeros((1, LANES - HALO), jnp.int32)], 1))
    sent_rows = jnp.concatenate([up[:HALO], down[:HALO]], 0)
    halo[SENT:, :] = jnp.zeros((TABLE - SENT, WIDTH), bf16)
    halo_new[SENT:, :] = jnp.zeros((TABLE - SENT, WIDTH), bf16)
    ready("lat")
    chosen[...] = dot(one_hot(sent_rows, 0, NODES // LANES), lat[...]).astype(bf16)

    pl.semaphore_wait(barrier, MEMBERS + 1)

    def exchange(source, into, send, recv):
        copies = []
        for i, neighbour in enumerate((above, below)):
            copy = pltpu.make_async_remote_copy(
                src_ref=source.at[pl.ds(i * HALO, HALO)],
                dst_ref=into.at[pl.ds(i * HALO, HALO)],
                send_sem=send.at[i],
                recv_sem=recv.at[i],
                device_id=(member, neighbour),
                device_id_type=MESH,
            )
            copy.start()
            copies.append(copy)
        return copies

    first = exchange(chosen, halo, send_sem, recv_sem)

    ready("ws", "wr", "es", "er")
    wp[pl.ds(WIDTH, WIDTH), :] = dot(lat[...], ws[...]).astype(bf16)
    wp[pl.ds(2 * WIDTH, WIDTH), :] = dot(lat[...], wr[...]).astype(bf16)
    count = count_s[0]
    slots = (
        lax.broadcasted_iota(jnp.int32, (EDGES // LANES, LANES), 0) * LANES
        + lax.broadcasted_iota(jnp.int32, (EDGES // LANES, LANES), 1)
    )
    live[...] = jnp.where(slots < count, er[...], -1)
    ready("we", "elat")

    def edge_rows(t, indices):
        each = EDGE_TILE // LANES
        return jnp.concatenate(
            [spread(indices[pl.ds(t * each + i, 1), :]) for i in range(each)], 0
        )

    for t in range(EDGES // EDGE_TILE):
        rows = pl.ds(t * EDGE_TILE, EDGE_TILE)
        picks = [
            elat[rows, :],
            one_hot(edge_rows(t, es), 0, NODES // LANES),
            one_hot(edge_rows(t, er), 0, NODES // LANES),
        ]
        acc[rows, :] = dot(jnp.concatenate(picks, 1), wp[...])
    ready("eo")
    eo[...] = centre(eo[...])
    for copy in first:
        copy.wait()

    table[...] = dot(halo[...], ws[...]).astype(bf16)
    for t in range(EDGES // EDGE_TILE):
        rows = pl.ds(t * EDGE_TILE, EDGE_TILE)
        inner = silu(
            acc[rows, :] + dot(one_hot(edge_rows(t, es), NODES, TABLE // LANES), table[...])
        )
        outer = dot(inner, eo[...])
        message[rows, :] = (outer * inverse_spread(outer)).astype(bf16)

    ready("ni", "no")
    no[...] = centre(no[...])

    def node_update(latent, placing):
        summed = dot(placing, message[...]).astype(bf16)
        inner = silu(dot(jnp.concatenate([latent, summed], 1), ni[...]))
        outer = dot(inner, no[...])
        return (latent.astype(f32) + outer * inverse_spread(outer)).astype(bf16)

    def placing(nodes):
        blocks = [
            jnp.where(nodes == live[i : i + 1, :], 1.0, 0.0).astype(bf16)
            for i in range(EDGES // LANES)
        ]
        return jnp.concatenate(blocks, 1)

    chosen_new[...] = node_update(chosen[...], placing(sent_rows))
    second = exchange(chosen_new, halo_new, send_new_sem, recv_new_sem)

    for t in range(NODES // NODE_TILE):
        rows = pl.ds(t * NODE_TILE, NODE_TILE)
        nodes = lax.broadcasted_iota(jnp.int32, (NODE_TILE, LANES), 0) + t * NODE_TILE
        updated[rows, :] = node_update(lat[rows, :], placing(nodes))
    ready("gws", "gwe", "gs", "glat")
    gwp[pl.ds(WIDTH, WIDTH), :] = dot(updated[...], gws[...]).astype(bf16)

    def grid_rows(t):
        each = GRID_TILE // LANES
        return jnp.concatenate([spread(gs[pl.ds(t * each + i, 1), :]) for i in range(each)], 0)

    for t in range(DECODER // GRID_TILE):
        rows = pl.ds(t * GRID_TILE, GRID_TILE)
        picks = [glat[rows, :], one_hot(grid_rows(t), 0, NODES // LANES)]
        acc_grid[rows, :] = dot(jnp.concatenate(picks, 1), gwp[...])
    ready("go", "ow", "prior", "target", "cw", "aw")
    go[...] = centre(go[...])
    for copy in second:
        copy.wait()

    table[...] = dot(halo_new[...], gws[...]).astype(bf16)
    diff[pl.ds(PADDED - 16, 16), :] = jnp.zeros((16, POINTS), f32)
    for t in range(DECODER // GRID_TILE):
        rows = pl.ds(t * GRID_TILE, GRID_TILE)
        inner = silu(
            acc_grid[rows, :] + dot(one_hot(grid_rows(t), NODES, TABLE // LANES), table[...])
        )
        outer = dot(inner, go[...])
        channels = lax.dot_general(
            outer.astype(bf16), ow[...], (((1,), (1,)), ((), ())), preferred_element_type=f32
        )
        readout[rows, 0:CHANNELS] = channels * inverse_spread(outer)
        points = pl.ds(t * LANES, LANES)
        output = (
            readout[pl.ds(t * GRID_TILE, LANES, 3), :]
            + readout[pl.ds(t * GRID_TILE + 1, LANES, 3), :]
            + readout[pl.ds(t * GRID_TILE + 2, LANES, 3), :]
        )
        diff[0:CHANNELS, points] = (
            prior[:, points] + output.T[0:CHANNELS] - target[:, points]
        )
        for half in range(2):
            outgoing[2 * t + half] = diff[pl.ds(half * HALF, HALF), points].astype(bf16)

    sent = []
    for k in range(1, MEMBERS):
        peer = lax.rem(member + k, MEMBERS)
        copy = pltpu.make_async_remote_copy(
            src_ref=outgoing.at[peer],
            dst_ref=incoming.at[k],
            send_sem=out_sem.at[k],
            recv_sem=in_sem.at[k],
            device_id=(peer, band),
            device_id_type=MESH,
        )
        copy.start()
        sent.append(copy)
    incoming[0] = outgoing[member]
    for copy in sent:
        copy.wait()
    values = [incoming[k].astype(f32) for k in range(MEMBERS)]
    sums = [None] * MEMBERS
    for m in range(MEMBERS):
        for n in range(m):
            term = slope(values[m] - values[n])
            sums[m] = term if sums[m] is None else sums[m] + term
            sums[n] = -term if sums[n] is None else sums[n] - term
    for m in range(MEMBERS):
        pairs[m] = sums[m].astype(bf16)
    sent = []
    for k in range(1, MEMBERS):
        owner = lax.rem(member + MEMBERS - k, MEMBERS)
        copy = pltpu.make_async_remote_copy(
            src_ref=pairs.at[k],
            dst_ref=answers.at[member],
            send_sem=back_sem.at[k],
            recv_sem=answer_sem.at[k],
            device_id=(owner, band),
            device_id_type=MESH,
        )
        copy.start()
        sent.append(copy)
    answers[member] = pairs[0]
    gains = spread(
        jnp.concatenate([cw[...], jnp.zeros((1, LANES - CHANNELS), f32)], 1)
    )
    for copy in sent:
        copy.wait()
    for t in range(POINTS // LANES):
        points = pl.ds(t * LANES, LANES)
        pairwise = jnp.concatenate(
            [answers[2 * t].astype(f32), answers[2 * t + 1].astype(f32)], 0
        )
        result = slope(diff[:, points]) - pairwise * (1.0 / (MEMBERS - 1))
        result = result * gains[:PADDED] * aw[t : t + 1, :]
        out_ref[0, :, points] = result[0:CHANNELS]


def per_device(
    mesh_latent, edge_latent, grid_edge_latent, edge_inner, edge_outer, node_inner, node_outer,
    grid_inner, grid_outer, out_weight, prior_state, target, channel_weight, area_weight,
    send_rows, edge_senders, edge_receivers, edge_count, grid_senders,
):
    hbm = pl.BlockSpec(memory_space=pl.ANY)
    dma = pltpu.SemaphoreType.DMA
    vmem = pltpu.VMEM
    square = vmem((WIDTH, WIDTH), bf16)
    scratch = [
        square,
        vmem((EDGES, WIDTH), bf16),
        vmem((DECODER, WIDTH), bf16),
        square,
        square,
        vmem((3 * WIDTH, WIDTH), bf16),
        square,
        vmem((2 * WIDTH, WIDTH), bf16),
        square,
        square,
        vmem((2 * WIDTH, WIDTH), bf16),
        square,
        vmem((CHANNELS, WIDTH), bf16),
        vmem((CHANNELS, POINTS), f32),
        vmem((CHANNELS, POINTS), f32),
        vmem((1, CHANNELS), f32),
        vmem((POINTS // LANES, LANES), f32),
        vmem((2, HALO), jnp.int32),
        vmem((EDGES // LANES, LANES), jnp.int32),
        vmem((EDGES // LANES, LANES), jnp.int32),
        vmem((DECODER // LANES, LANES), jnp.int32),
        vmem((SENT, WIDTH), bf16),
        vmem((TABLE, WIDTH), bf16),
        vmem((SENT, WIDTH), bf16),
        vmem((TABLE, WIDTH), bf16),
        vmem((TABLE, WIDTH), bf16),
        vmem((EDGES, WIDTH), f32),
        vmem((DECODER, WIDTH), f32),
        vmem((EDGES // LANES, LANES), jnp.int32),
        vmem((EDGES, WIDTH), bf16),
        vmem((NODES, WIDTH), bf16),
        vmem((DECODER, LANES), f32),
        vmem((PADDED, POINTS), f32),
        vmem((MEMBERS, HALF, LANES), bf16),
        vmem((MEMBERS, HALF, LANES), bf16),
        vmem((MEMBERS, HALF, LANES), bf16),
        vmem((MEMBERS, HALF, LANES), bf16),
        dma((21,)),
        dma((2,)),
        dma((2,)),
        dma((2,)),
        dma((2,)),
        dma((MEMBERS,)),
        dma((MEMBERS,)),
        dma((MEMBERS,)),
        dma((MEMBERS,)),
    ]
    return pl.pallas_call(
        kernel,
        out_shape=jax.ShapeDtypeStruct((1, CHANNELS, POINTS), f32),
        in_specs=[hbm] * 18 + [pl.BlockSpec(memory_space=pltpu.SMEM)],
        out_specs=pl.BlockSpec(memory_space=pltpu.VMEM),
        scratch_shapes=scratch,
        compiler_params=pltpu.CompilerParams(
            collective_id=0, has_side_effects=True, vmem_limit_bytes=48 * 1024 * 1024
        ),
        cost_estimate=pl.CostEstimate(
            flops=9_000_000_000, bytes_accessed=9_000_000, transcendentals=2_000_000
        ),
        name="ensemble_layers",
    )(
        mesh_latent, edge_latent, grid_edge_latent, edge_inner, edge_outer, node_inner, node_outer,
        grid_inner, grid_outer, out_weight, prior_state, target,
        channel_weight.reshape(1, CHANNELS),
        area_weight.reshape(POINTS // LANES, LANES),
        send_rows,
        edge_senders.reshape(EDGES // LANES, LANES),
        edge_receivers.reshape(EDGES // LANES, LANES),
        grid_senders.reshape(DECODER // LANES, LANES),
        edge_count,
    )


def solution(mesh):
    in_specs = (
        P("mem", "patch", None),
        P("patch", None),
        P("patch", None),
        P(),
        P(),
        P(),
        P(),
        P(),
        P(),
        P(),
        P(None, "patch"),
        P(None, "patch"),
        P(),
        P("patch"),
        P("patch", None, None),
        P("patch"),
        P("patch"),
        P("patch"),
        P("patch"),
    )
    out_specs = P("mem", None, "patch")
    return jax.shard_map(
        per_device, mesh=mesh, in_specs=in_specs, out_specs=out_specs, check_vma=False
    )
```

time: 93.4 us -> 51.7 us (0.55)
  the two profiles are of different devices: /device:TPU:7 before, /device:TPU:1 now
where the time goes in v1:
time: 51.7 us; the launch traced here: 51.1 us
  Pallas kernels  34.9 us (68%)
  local copies, waits for them, and re-layouts  15.5 us (30%)
  between operations  0.68 us (1%)
    pallas_call x1, Pallas kernels, per_device(): pl.pallas_call(kernel, out_shape=jax.ShapeDtypeStruct((1, CHANNELS, POINT...  34.9 us
    unnamed x32, local copies, waits for them, and re-layouts  14.6 us

profile of v1, /device:TPU:1, one launch (start us, length us, event | category | flops | bytes accessed | tf_op | source)
XLA Modules:
  0.0 51.1 jit_solution(3918710918731158420)
XLA Ops:
  0.7 0.0 copy-start
  0.7 1.2 %copy-done = bf16[1024,512]{1,0:T(8,128)(2,1)S(1)} copy-done((bf16[1024,512]{1,0:T(8,128)(2,1)S(1)}, bf16[1024,512]{1,0:T(8,128)(2,1)}, u32[]{:S(2)}) %copy-start) | copy-done | bytes 1048600
  1.9 0.0 copy-start.1
  1.9 1.2 %copy-done.1 = bf16[1024,512]{1,0:T(8,128)(2,1)S(1)} copy-done((bf16[1024,512]{1,0:T(8,128)(2,1)S(1)}, bf16[1024,512]{1,0:T(8,128)(2,1)}, u32[]{:S(2)}) %copy-start.1) | copy-done | bytes 1048600
  3.1 0.0 copy-start.2
  3.1 1.2 %copy-done.2 = bf16[1024,512]{1,0:T(8,128)(2,1)S(1)} copy-done((bf16[1024,512]{1,0:T(8,128)(2,1)S(1)}, bf16[1024,512]{1,0:T(8,128)(2,1)}, u32[]{:S(2)}) %copy-start.2) | copy-done | bytes 1048600
  4.3 0.0 copy-start.3
  4.3 1.0 %copy-done.3 = bf16[1,512,512]{2,1,0:T(8,128)(2,1)S(1)} copy-done((bf16[1,512,512]{2,1,0:T(8,128)(2,1)S(1)}, bf16[1,512,512]{2,1,0:T(8,128)(2,1)}, u32[]{:S(2)}) %copy-start.3) | copy-done | bytes 524312
  5.4 0.0 copy-start.4
  5.4 1.0 %copy-done.4 = bf16[512,512]{1,0:T(8,128)(2,1)S(1)} copy-done((bf16[512,512]{1,0:T(8,128)(2,1)S(1)}, bf16[512,512]{1,0:T(8,128)(2,1)}, u32[]{:S(2)}) %copy-start.4) | copy-done | bytes 524312
  6.4 0.0 copy-start.5
  6.4 1.0 %copy-done.5 = bf16[512,512]{1,0:T(8,128)(2,1)S(1)} copy-done((bf16[512,512]{1,0:T(8,128)(2,1)S(1)}, bf16[512,512]{1,0:T(8,128)(2,1)}, u32[]{:S(2)}) %copy-start.5) | copy-done | bytes 524312
  7.5 0.0 copy-start.6
  7.5 1.0 %copy-done.6 = bf16[512,512]{1,0:T(8,128)(2,1)S(1)} copy-done((bf16[512,512]{1,0:T(8,128)(2,1)S(1)}, bf16[512,512]{1,0:T(8,128)(2,1)}, u32[]{:S(2)}) %copy-start.6) | copy-done | bytes 524312
  8.5 0.0 copy-start.7
  8.5 0.9 %copy-done.7 = f32[87,512]{1,0:T(8,128)S(1)} copy-done((f32[87,512]{1,0:T(8,128)S(1)}, f32[87,512]{1,0:T(8,128)}, u32[]{:S(2)}) %copy-start.7) | copy-done | bytes 178200
  9.4 0.0 copy-start.8
  9.4 0.9 %copy-done.8 = f32[87,512]{1,0:T(8,128)S(1)} copy-done((f32[87,512]{1,0:T(8,128)S(1)}, f32[87,512]{1,0:T(8,128)}, u32[]{:S(2)}) %copy-start.8) | copy-done | bytes 178200
  10.3 0.0 copy-start.9
  10.3 0.9 %copy-done.9 = bf16[87,512]{1,0:T(8,128)(2,1)S(1)} copy-done((bf16[87,512]{1,0:T(8,128)(2,1)S(1)}, bf16[87,512]{1,0:T(8,128)(2,1)}, u32[]{:S(2)}) %copy-start.9) | copy-done | bytes 89112
  11.2 0.0 copy-start.10
  11.2 0.7 %copy-done.10 = s32[1536]{0:T(1024)S(1)} copy-done((s32[1536]{0:T(1024)S(1)}, s32[1536]{0:T(1024)}, u32[]{:S(2)}) %copy-start.10) | copy-done | bytes 6168
  11.9 0.0 copy-start.11
  11.9 0.7 %copy-done.11 = s32[1024]{0:T(1024)S(1)} copy-done((s32[1024]{0:T(1024)S(1)}, s32[1024]{0:T(1024)}, u32[]{:S(2)}) %copy-start.11) | copy-done | bytes 4120
  12.6 0.0 copy-start.12
  12.6 0.7 %copy-done.12 = s32[1024]{0:T(1024)S(1)} copy-done((s32[1024]{0:T(1024)S(1)}, s32[1024]{0:T(1024)}, u32[]{:S(2)}) %copy-start.12) | copy-done | bytes 4120
  13.3 0.0 copy-start.13
  13.3 0.7 %copy-done.13 = f32[512]{0:T(512)S(1)} copy-done((f32[512]{0:T(512)S(1)}, f32[512]{0:T(512)}, u32[]{:S(2)}) %copy-start.13) | copy-done | bytes 2072
  14.0 0.0 copy-start.14
  14.0 0.7 %copy-done.14 = s32[1,2,96]{2,1,0:T(2,128)S(1)} copy-done((s32[1,2,96]{2,1,0:T(2,128)S(1)}, s32[1,2,96]{2,1,0:T(2,128)}, u32[]{:S(2)}) %copy-start.14) | copy-done | bytes 792
  14.7 0.0 copy-start.15
  14.7 0.7 %copy-done.15 = f32[87]{0:T(128)S(1)} copy-done((f32[87]{0:T(128)S(1)}, f32[87]{0:T(128)}, u32[]{:S(2)}) %copy-start.15) | copy-done | bytes 372
  15.3 34.9 %ensemble_layers.1 = f32[1,87,512]{2,1,0:T(8,128)S(1)} custom-call(bf16[1,512,512]{2,1,0:T(8,128)(2,1)S(1)} %copy-done.3, bf16[1024,512]{1,0:T(8,128)(2,1)S(1)} %copy-done, bf16[1536,512]{1,0:T(8,128)(2,1)} %glat_h.1, bf16[1536,512]{1,0:T(8,128)(2,1)} %ei_h.1, bf16[512,512]{1,0:T(8,128)(2,1)S(1)} %copy-done.4, bf16[1024,512]{1,0:T(8,128)(2,1)S(1)} %copy-done.1, ...), custom_call_target="tpu_custom_call" | custom-call | flops 8999999488 | bytes 9000000 | tf_op jit(solution)/shard_map/ensemble_layers/pallas_call | solution.py:364
  50.2 0.9 %copy.20 = f32[1,87,512]{2,0,1:T(1,128)} copy(f32[1,87,512]{2,1,0:T(8,128)S(1)} %ensemble_layers.1) | data formatting | bytes 356352 | tf_op jit(solution)/shard_map/ensemble_layers/pallas_call | solution.py:364
Async XLA Ops:
  0.7 1.2 %copy-start = (bf16[1024,512]{1,0:T(8,128)(2,1)S(1)}, bf16[1024,512]{1,0:T(8,128)(2,1)}, u32[]{:S(2)}) copy-start(bf16[1024,512]{1,0:T(8,128)(2,1)} %elat_h.1) | copy-start | bytes 3145732
  1.9 1.2 %copy-start.1 = (bf16[1024,512]{1,0:T(8,128)(2,1)S(1)}, bf16[1024,512]{1,0:T(8,128)(2,1)}, u32[]{:S(2)}) copy-start(bf16[1024,512]{1,0:T(8,128)(2,1)} %ni_h.1) | copy-start | bytes 3145732
  3.1 1.2 %copy-start.2 = (bf16[1024,512]{1,0:T(8,128)(2,1)S(1)}, bf16[1024,512]{1,0:T(8,128)(2,1)}, u32[]{:S(2)}) copy-start(bf16[1024,512]{1,0:T(8,128)(2,1)} %gi_h.1) | copy-start | bytes 3145732
  4.3 1.0 %copy-start.3 = (bf16[1,512,512]{2,1,0:T(8,128)(2,1)S(1)}, bf16[1,512,512]{2,1,0:T(8,128)(2,1)}, u32[]{:S(2)}) copy-start(bf16[1,512,512]{2,1,0:T(8,128)(2,1)} %lat_h.1) | copy-start | bytes 1572868
  5.4 1.0 %copy-start.4 = (bf16[512,512]{1,0:T(8,128)(2,1)S(1)}, bf16[512,512]{1,0:T(8,128)(2,1)}, u32[]{:S(2)}) copy-start(bf16[512,512]{1,0:T(8,128)(2,1)} %eo_h.1) | copy-start | bytes 1572868
  6.4 1.0 %copy-start.5 = (bf16[512,512]{1,0:T(8,128)(2,1)S(1)}, bf16[512,512]{1,0:T(8,128)(2,1)}, u32[]{:S(2)}) copy-start(bf16[512,512]{1,0:T(8,128)(2,1)} %no_h.1) | copy-start | bytes 1572868
  7.5 1.0 %copy-start.6 = (bf16[512,512]{1,0:T(8,128)(2,1)S(1)}, bf16[512,512]{1,0:T(8,128)(2,1)}, u32[]{:S(2)}) copy-start(bf16[512,512]{1,0:T(8,128)(2,1)} %go_h.1) | copy-start | bytes 1572868
  8.5 0.9 %copy-start.7 = (f32[87,512]{1,0:T(8,128)S(1)}, f32[87,512]{1,0:T(8,128)}, u32[]{:S(2)}) copy-start(f32[87,512]{1,0:T(8,128)} %prior_h.1) | copy-start | bytes 534532
  9.4 0.9 %copy-start.8 = (f32[87,512]{1,0:T(8,128)S(1)}, f32[87,512]{1,0:T(8,128)}, u32[]{:S(2)}) copy-start(f32[87,512]{1,0:T(8,128)} %target_h.1) | copy-start | bytes 534532
  10.3 0.9 %copy-start.9 = (bf16[87,512]{1,0:T(8,128)(2,1)S(1)}, bf16[87,512]{1,0:T(8,128)(2,1)}, u32[]{:S(2)}) copy-start(bf16[87,512]{1,0:T(8,128)(2,1)} %ow_h.1) | copy-start | bytes 267268
  11.2 0.7 %copy-start.10 = (s32[1536]{0:T(1024)S(1)}, s32[1536]{0:T(1024)}, u32[]{:S(2)}) copy-start(s32[1536]{0:T(1024)} %param.37) | copy-start | bytes 18436
  11.9 0.7 %copy-start.11 = (s32[1024]{0:T(1024)S(1)}, s32[1024]{0:T(1024)}, u32[]{:S(2)}) copy-start(s32[1024]{0:T(1024)} %param.34) | copy-start | bytes 12292
  12.6 0.7 %copy-start.12 = (s32[1024]{0:T(1024)S(1)}, s32[1024]{0:T(1024)}, u32[]{:S(2)}) copy-start(s32[1024]{0:T(1024)} %param.35) | copy-start | bytes 12292
  13.3 0.7 %copy-start.13 = (f32[512]{0:T(512)S(1)}, f32[512]{0:T(512)}, u32[]{:S(2)}) copy-start(f32[512]{0:T(512)} %param.32) | copy-start | bytes 6148
  14.0 0.7 %copy-start.14 = (s32[1,2,96]{2,1,0:T(2,128)S(1)}, s32[1,2,96]{2,1,0:T(2,128)}, u32[]{:S(2)}) copy-start(s32[1,2,96]{2,1,0:T(2,128)} %sends_h.1) | copy-start | bytes 2308
  14.7 0.7 %copy-start.15 = (f32[87]{0:T(128)S(1)}, f32[87]{0:T(128)}, u32[]{:S(2)}) copy-start(f32[87]{0:T(128)} %param.31) | copy-start | bytes 1048

commit v2 on v1

--- a/solution.py
+++ b/solution.py
@@ -23,8 +23,10 @@
 POINTS = 512
 CHANNELS = 87
 PADDED = 96
-HALF = 48
 MEMBERS = 8
+PEERS = 3
+CHUNKS = 2
+CHUNK = POINTS // CHUNKS
 EDGE_TILE = 256
 GRID_TILE = 384
 NODE_TILE = 256
@@ -67,18 +69,39 @@
 
 def kernel(
     lat_h, elat_h, glat_h, ei_h, eo_h, ni_h, no_h, gi_h, go_h, ow_h, prior_h, target_h,
-    cw_h, aw_h, sends_h, es_h, er_h, gs_h, count_s,
+    cw_h, aw_h, sends_h, es_h, er_h, gs_h, count_h,
     out_ref,
-    lat, elat, glat, ws, wr, wp, eo, ni, no, gws, gwp, go, ow, prior, target, cw, aw, sends, es, er, gs,
+    lat, elat, glat, ws, wr, wp, eo, ni, no, gws, gwp, go, ow, prior, target, cw, aw, sends, es, er, gs, count,
     chosen, halo, chosen_new, halo_new, table, acc, acc_grid, live, message, updated, readout,
-    diff, outgoing, incoming, pairs, answers,
-    load_sem, send_sem, recv_sem, send_new_sem, recv_new_sem, out_sem, in_sem, back_sem, answer_sem,
+    diff, outgoing, incoming, beside, pairwise, partial, partial_in,
+    load_sem, send_sem, recv_sem, send_new_sem, recv_new_sem, peer_sem, peer_in_sem, beside_sem, beside_in_sem,
+    partial_sem, partial_in_sem,
 ):
     member = lax.axis_index("mem")
     band = lax.axis_index("patch")
     bands = lax.axis_size("patch")
-    above = lax.rem(band + 1, bands)
-    below = lax.rem(band + bands - 1, bands)
+    above = band + 1
+    below = band - 1
+    has_above = band < bands - 1
+    has_below = band > 0
+    sibling = member + 1 - 2 * lax.rem(member, 2)
+    peers = [lax.rem(member + 2 * k, MEMBERS) for k in range(1, PEERS + 1)]
+
+    barrier = pltpu.get_barrier_semaphore()
+
+    def greet(other, row):
+        pl.semaphore_signal(barrier, inc=1, device_id=(other, row), device_id_type=MESH)
+
+    @pl.when(has_above)
+    def _():
+        greet(member, above)
+
+    @pl.when(has_below)
+    def _():
+        greet(member, below)
+
+    for other in peers + [sibling]:
+        greet(other, band)
 
     loads = {}
 
@@ -97,8 +120,70 @@
     load("wr", ei_h.at[pl.ds(WIDTH, WIDTH)], wr)
     load("es", es_h, es)
     load("er", er_h, er)
+    load("count", count_h, count)
     load("we", ei_h.at[pl.ds(2 * WIDTH, WIDTH)], wp.at[pl.ds(0, WIDTH)])
     load("elat", elat_h, elat)
+    ready("sends")
+    up = spread(jnp.concatenate([sends[0:1, :], jnp.zeros((1, LANES - HALO), jnp.int32)], 1))
+    down = spread(jnp.concatenate([sends[1:2, :], jnp.zeros((1, LANES - HALO), jnp.int32)], 1))
+    sent_rows = jnp.concatenate([up[:HALO], down[:HALO]], 0)
+    for rows in (halo, halo_new):
+        rows[SENT:, :] = jnp.zeros((TABLE - SENT, WIDTH), bf16)
+
+        @pl.when(jnp.logical_not(has_below))
+        def _():
+            rows[:HALO, :] = jnp.zeros((HALO, WIDTH), bf16)
+
+        @pl.when(jnp.logical_not(has_above))
+        def _():
+            rows[HALO:SENT, :] = jnp.zeros((HALO, WIDTH), bf16)
+
+    ready("lat")
+    chosen[...] = dot(one_hot(sent_rows, 0, NODES // LANES), lat[...]).astype(bf16)
+
+    pl.semaphore_wait(
+        barrier, PEERS + 1 + has_above.astype(jnp.int32) + has_below.astype(jnp.int32)
+    )
+
+    def remote(source, into, send, recv, other, row):
+        return pltpu.make_async_remote_copy(
+            src_ref=source,
+            dst_ref=into,
+            send_sem=send,
+            recv_sem=recv,
+            device_id=(other, row),
+            device_id_type=MESH,
+        )
+
+    def exchange(source, into, send, recv):
+        copies = []
+        for i, (there, neighbour) in enumerate(((has_above, above), (has_below, below))):
+            part = pl.ds(i * HALO, HALO)
+            copy = remote(source.at[part], into.at[part], send.at[i], recv.at[i], member, neighbour)
+            copies.append(copy)
+
+            @pl.when(there)
+            def _():
+                copy.start()
+
+        return copies
+
+    def arrived(copies):
+        for copy, there in zip(copies, (has_below, has_above)):
+
+            @pl.when(there)
+            def _():
+                copy.wait_recv()
+
+    def left(copies):
+        for copy, there in zip(copies, (has_above, has_below)):
+
+            @pl.when(there)
+            def _():
+                copy.wait_send()
+
+    first = exchange(chosen, halo, send_sem, recv_sem)
+
     load("eo", eo_h, eo)
     load("ni", ni_h, ni)
     load("no", no_h, no)
@@ -112,51 +197,14 @@
     load("target", target_h, target)
     load("cw", cw_h, cw)
     load("aw", aw_h, aw)
-
-    barrier = pltpu.get_barrier_semaphore()
-    for neighbour in (above, below):
-        pl.semaphore_signal(barrier, inc=1, device_id=(member, neighbour), device_id_type=MESH)
-    for k in range(1, MEMBERS):
-        peer = lax.rem(member + k, MEMBERS)
-        pl.semaphore_signal(barrier, inc=1, device_id=(peer, band), device_id_type=MESH)
-
-    ready("sends")
-    up = spread(jnp.concatenate([sends[0:1, :], jnp.zeros((1, LANES - HALO), jnp.int32)], 1))
-    down = spread(jnp.concatenate([sends[1:2, :], jnp.zeros((1, LANES - HALO), jnp.int32)], 1))
-    sent_rows = jnp.concatenate([up[:HALO], down[:HALO]], 0)
-    halo[SENT:, :] = jnp.zeros((TABLE - SENT, WIDTH), bf16)
-    halo_new[SENT:, :] = jnp.zeros((TABLE - SENT, WIDTH), bf16)
-    ready("lat")
-    chosen[...] = dot(one_hot(sent_rows, 0, NODES // LANES), lat[...]).astype(bf16)
-
-    pl.semaphore_wait(barrier, MEMBERS + 1)
-
-    def exchange(source, into, send, recv):
-        copies = []
-        for i, neighbour in enumerate((above, below)):
-            copy = pltpu.make_async_remote_copy(
-                src_ref=source.at[pl.ds(i * HALO, HALO)],
-                dst_ref=into.at[pl.ds(i * HALO, HALO)],
-                send_sem=send.at[i],
-                recv_sem=recv.at[i],
-                device_id=(member, neighbour),
-                device_id_type=MESH,
-            )
-            copy.start()
-            copies.append(copy)
-        return copies
-
-    first = exchange(chosen, halo, send_sem, recv_sem)
-
-    ready("ws", "wr", "es", "er")
+    ready("ws", "wr", "es", "er", "count")
     wp[pl.ds(WIDTH, WIDTH), :] = dot(lat[...], ws[...]).astype(bf16)
     wp[pl.ds(2 * WIDTH, WIDTH), :] = dot(lat[...], wr[...]).astype(bf16)
-    count = count_s[0]
     slots = (
         lax.broadcasted_iota(jnp.int32, (EDGES // LANES, LANES), 0) * LANES
         + lax.broadcasted_iota(jnp.int32, (EDGES // LANES, LANES), 1)
     )
-    live[...] = jnp.where(slots < count, er[...], -1)
+    live[...] = jnp.where(slots < count[...], er[...], -1)
     ready("we", "elat")
 
     def edge_rows(t, indices):
@@ -175,8 +223,7 @@
         acc[rows, :] = dot(jnp.concatenate(picks, 1), wp[...])
     ready("eo")
     eo[...] = centre(eo[...])
-    for copy in first:
-        copy.wait()
+    arrived(first)
 
     table[...] = dot(halo[...], ws[...]).astype(bf16)
     for t in range(EDGES // EDGE_TILE):
@@ -223,11 +270,11 @@
         acc_grid[rows, :] = dot(jnp.concatenate(picks, 1), gwp[...])
     ready("go", "ow", "prior", "target", "cw", "aw")
     go[...] = centre(go[...])
-    for copy in second:
-        copy.wait()
+    arrived(second)
 
     table[...] = dot(halo_new[...], gws[...]).astype(bf16)
     diff[pl.ds(PADDED - 16, 16), :] = jnp.zeros((16, POINTS), f32)
+    to_peers, to_sibling, to_partial = [], [], []
     for t in range(DECODER // GRID_TILE):
         rows = pl.ds(t * GRID_TILE, GRID_TILE)
         inner = silu(
@@ -247,61 +294,68 @@
         diff[0:CHANNELS, points] = (
             prior[:, points] + output.T[0:CHANNELS] - target[:, points]
         )
-        for half in range(2):
-            outgoing[2 * t + half] = diff[pl.ds(half * HALF, HALF), points].astype(bf16)
-
-    sent = []
-    for k in range(1, MEMBERS):
-        peer = lax.rem(member + k, MEMBERS)
-        copy = pltpu.make_async_remote_copy(
-            src_ref=outgoing.at[peer],
-            dst_ref=incoming.at[k],
-            send_sem=out_sem.at[k],
-            recv_sem=in_sem.at[k],
-            device_id=(peer, band),
-            device_id_type=MESH,
-        )
-        copy.start()
-        sent.append(copy)
-    incoming[0] = outgoing[member]
-    for copy in sent:
-        copy.wait()
-    values = [incoming[k].astype(f32) for k in range(MEMBERS)]
-    sums = [None] * MEMBERS
-    for m in range(MEMBERS):
-        for n in range(m):
-            term = slope(values[m] - values[n])
-            sums[m] = term if sums[m] is None else sums[m] + term
-            sums[n] = -term if sums[n] is None else sums[n] - term
-    for m in range(MEMBERS):
-        pairs[m] = sums[m].astype(bf16)
-    sent = []
-    for k in range(1, MEMBERS):
-        owner = lax.rem(member + MEMBERS - k, MEMBERS)
-        copy = pltpu.make_async_remote_copy(
-            src_ref=pairs.at[k],
-            dst_ref=answers.at[member],
-            send_sem=back_sem.at[k],
-            recv_sem=answer_sem.at[k],
-            device_id=(owner, band),
-            device_id_type=MESH,
-        )
-        copy.start()
-        sent.append(copy)
-    answers[member] = pairs[0]
+        chunk, part = divmod(t * LANES, CHUNK)
+        outgoing[chunk, :, pl.ds(part, LANES)] = diff[:, points].astype(bf16)
+        if part + LANES == CHUNK:
+            to_peers.append([
+                remote(
+                    outgoing.at[chunk], incoming.at[chunk, k], peer_sem.at[chunk, k],
+                    peer_in_sem.at[chunk, k], peers[k], band,
+                )
+                for k in (1, 0, 2)
+            ])
+            to_sibling.append(
+                remote(
+                    outgoing.at[chunk], beside.at[chunk], beside_sem.at[chunk],
+                    beside_in_sem.at[chunk], sibling, band,
+                )
+            )
+            for copy in to_peers[-1] + to_sibling[-1:]:
+                copy.start()
+
     gains = spread(
         jnp.concatenate([cw[...], jnp.zeros((1, LANES - CHANNELS), f32)], 1)
     )
-    for copy in sent:
-        copy.wait()
-    for t in range(POINTS // LANES):
-        points = pl.ds(t * LANES, LANES)
-        pairwise = jnp.concatenate(
-            [answers[2 * t].astype(f32), answers[2 * t + 1].astype(f32)], 0
-        )
-        result = slope(diff[:, points]) - pairwise * (1.0 / (MEMBERS - 1))
-        result = result * gains[:PADDED] * aw[t : t + 1, :]
-        out_ref[0, :, points] = result[0:CHANNELS]
+    blocks = [pl.ds(part, LANES) for part in range(0, CHUNK, LANES)]
+    for chunk in range(CHUNKS):
+        to_sibling[chunk].wait_recv()
+        for copy in to_peers[chunk]:
+            copy.wait_recv()
+        for block in blocks:
+            near = beside[chunk, :, block].astype(f32)
+            total = None
+            for k in range(PEERS):
+                term = slope(near - incoming[chunk, k, :, block].astype(f32))
+                total = term if total is None else total + term
+            partial[chunk, :, block] = total.astype(bf16)
+        copy = remote(
+            partial.at[chunk], partial_in.at[chunk], partial_sem.at[chunk],
+            partial_in_sem.at[chunk], sibling, band,
+        )
+        copy.start()
+        to_partial.append(copy)
+        for block in blocks:
+            points = pl.ds(chunk * CHUNK + block.start, LANES)
+            own = diff[:, points]
+            total = slope(own - beside[chunk, :, block].astype(f32))
+            for k in range(PEERS):
+                total = total + slope(own - incoming[chunk, k, :, block].astype(f32))
+            pairwise[:, points] = slope(own) - total * (1.0 / (MEMBERS - 1))
+    for chunk in range(CHUNKS):
+        to_partial[chunk].wait_recv()
+        for block in blocks:
+            points = pl.ds(chunk * CHUNK + block.start, LANES)
+            t = (chunk * CHUNK + block.start) // LANES
+            result = pairwise[:, points] - partial_in[chunk, :, block].astype(f32) * (
+                1.0 / (MEMBERS - 1)
+            )
+            result = result * gains[:PADDED] * aw[t : t + 1, :]
+            out_ref[0, :, points] = result[0:CHANNELS]
+    left(first)
+    left(second)
+    for chunk in range(CHUNKS):
+        for copy in to_peers[chunk] + [to_sibling[chunk], to_partial[chunk]]:
+            copy.wait_send()
 
 
 def per_device(
@@ -309,7 +363,7 @@
     grid_inner, grid_outer, out_weight, prior_state, target, channel_weight, area_weight,
     send_rows, edge_senders, edge_receivers, edge_count, grid_senders,
 ):
-    hbm = pl.BlockSpec(memory_space=pl.ANY)
+    hbm = pl.BlockSpec(memory_space=pltpu.HBM)
     dma = pltpu.SemaphoreType.DMA
     vmem = pltpu.VMEM
     square = vmem((WIDTH, WIDTH), bf16)
@@ -335,6 +389,7 @@
         vmem((EDGES // LANES, LANES), jnp.int32),
         vmem((EDGES // LANES, LANES), jnp.int32),
         vmem((DECODER // LANES, LANES), jnp.int32),
+        vmem((1, 1), jnp.int32),
         vmem((SENT, WIDTH), bf16),
         vmem((TABLE, WIDTH), bf16),
         vmem((SENT, WIDTH), bf16),
@@ -347,28 +402,32 @@
         vmem((NODES, WIDTH), bf16),
         vmem((DECODER, LANES), f32),
         vmem((PADDED, POINTS), f32),
-        vmem((MEMBERS, HALF, LANES), bf16),
-        vmem((MEMBERS, HALF, LANES), bf16),
-        vmem((MEMBERS, HALF, LANES), bf16),
-        vmem((MEMBERS, HALF, LANES), bf16),
-        dma((21,)),
+        vmem((CHUNKS, PADDED, CHUNK), bf16),
+        vmem((CHUNKS, PEERS, PADDED, CHUNK), bf16),
+        vmem((CHUNKS, PADDED, CHUNK), bf16),
+        vmem((PADDED, POINTS), f32),
+        vmem((CHUNKS, PADDED, CHUNK), bf16),
+        vmem((CHUNKS, PADDED, CHUNK), bf16),
+        dma((22,)),
         dma((2,)),
         dma((2,)),
         dma((2,)),
         dma((2,)),
-        dma((MEMBERS,)),
-        dma((MEMBERS,)),
-        dma((MEMBERS,)),
-        dma((MEMBERS,)),
+        dma((CHUNKS, PEERS)),
+        dma((CHUNKS, PEERS)),
+        dma((CHUNKS,)),
+        dma((CHUNKS,)),
+        dma((CHUNKS,)),
+        dma((CHUNKS,)),
     ]
     return pl.pallas_call(
         kernel,
         out_shape=jax.ShapeDtypeStruct((1, CHANNELS, POINTS), f32),
-        in_specs=[hbm] * 18 + [pl.BlockSpec(memory_space=pltpu.SMEM)],
+        in_specs=[hbm] * 19,
         out_specs=pl.BlockSpec(memory_space=pltpu.VMEM),
         scratch_shapes=scratch,
         compiler_params=pltpu.CompilerParams(
-            collective_id=0, has_side_effects=True, vmem_limit_bytes=48 * 1024 * 1024
+            collective_id=0, has_side_effects=True, vmem_limit_bytes=60 * 1024 * 1024
         ),
         cost_estimate=pl.CostEstimate(
             flops=9_000_000_000, bytes_accessed=9_000_000, transcendentals=2_000_000
@@ -383,7 +442,7 @@
         edge_senders.reshape(EDGES // LANES, LANES),
         edge_receivers.reshape(EDGES // LANES, LANES),
         grid_senders.reshape(DECODER // LANES, LANES),
-        edge_count,
+        edge_count.reshape(1, 1),
     )
 
 

time: 51.7 us -> 32.5 us (0.63)
  the two profiles are of different devices: /device:TPU:1 before, /device:TPU:7 now
where the time goes in v2:
time: 32.5 us; the launch traced here: 32.3 us
  Pallas kernels  29.9 us (92%)
  local copies, waits for them, and re-layouts  1.78 us (5%)
  between operations  0.66 us (2%)
    pallas_call x1, Pallas kernels, per_device(): pl.pallas_call(kernel, out_shape=jax.ShapeDtypeStruct((1, CHANNELS, POINT...  29.9 us
    pallas_call x1, local copies, waits for them, and re-layouts, per_device(): pl.pallas_call(kernel, out_shape=jax.ShapeDtypeStruct((1, CHANNELS, POINT...  1.78 us

profile of v2, /device:TPU:7, one launch (start us, length us, event | category | flops | bytes accessed | tf_op | source)
XLA Modules:
  0.0 32.3 jit_solution(8877973946713543296)
XLA Ops:
  0.7 29.9 %ensemble_layers.1 = f32[1,87,512]{2,1,0:T(8,128)} custom-call(bf16[1,512,512]{2,1,0:T(8,128)(2,1)} %lat_h.1, bf16[1024,512]{1,0:T(8,128)(2,1)} %elat_h.1, bf16[1536,512]{1,0:T(8,128)(2,1)} %glat_h.1, bf16[1536,512]{1,0:T(8,128)(2,1)} %ei_h.1, bf16[512,512]{1,0:T(8,128)(2,1)} %eo_h.1, bf16[1024,512]{1,0:T(8,128)(2,1)} %ni_h.1, bf16[512,512]{1,0:T(8,128)(2,1)} %no_h.1, ...), custom_call_target="tpu_custom_call" | custom-call | flops 8999999488 | bytes 9000000 | tf_op jit(solution)/shard_map/ensemble_layers/pallas_call | solution.py:423
  30.6 1.8 %copy.20 = f32[1,87,512]{2,0,1:T(1,128)} copy(f32[1,87,512]{2,1,0:T(8,128)} %ensemble_layers.1) | data formatting | bytes 356352 | tf_op jit(solution)/shard_map/ensemble_layers/pallas_call | solution.py:423

commit v3 on v2

--- a/solution.py
+++ b/solution.py
@@ -27,7 +27,7 @@
 PEERS = 3
 CHUNKS = 2
 CHUNK = POINTS // CHUNKS
-EDGE_TILE = 256
+EDGE_TILE = 512
 GRID_TILE = 384
 NODE_TILE = 256
 
@@ -42,8 +42,9 @@
 
 def one_hot(rows, base, blocks):
     lanes = lax.broadcasted_iota(jnp.int32, rows.shape, 1)
+    rows = rows.astype(jnp.int16)
     parts = [
-        jnp.where(rows == lanes + (base + LANES * b), 1.0, 0.0).astype(bf16)
+        jnp.where(rows == (lanes + (base + LANES * b)).astype(jnp.int16), jnp.ones((), bf16), jnp.zeros((), bf16))
         for b in range(blocks)
     ]
     return parts[0] if blocks == 1 else jnp.concatenate(parts, 1)
@@ -72,7 +73,7 @@
     cw_h, aw_h, sends_h, es_h, er_h, gs_h, count_h,
     out_ref,
     lat, elat, glat, ws, wr, wp, eo, ni, no, gws, gwp, go, ow, prior, target, cw, aw, sends, es, er, gs, count,
-    chosen, halo, chosen_new, halo_new, table, acc, acc_grid, live, message, updated, readout,
+    chosen, halo, chosen_new, halo_new, table, from_halo, into_sent, grid_from_halo, acc, acc_grid, live, message, updated, readout,
     diff, outgoing, incoming, beside, pairwise, partial, partial_in,
     load_sem, send_sem, recv_sem, send_new_sem, recv_new_sem, peer_sem, peer_in_sem, beside_sem, beside_in_sem,
     partial_sem, partial_in_sem,
@@ -215,33 +216,18 @@
 
     for t in range(EDGES // EDGE_TILE):
         rows = pl.ds(t * EDGE_TILE, EDGE_TILE)
+        senders = edge_rows(t, es)
+        from_halo[rows, :] = one_hot(senders, NODES, TABLE // LANES)
         picks = [
             elat[rows, :],
-            one_hot(edge_rows(t, es), 0, NODES // LANES),
+            one_hot(senders, 0, NODES // LANES),
             one_hot(edge_rows(t, er), 0, NODES // LANES),
         ]
         acc[rows, :] = dot(jnp.concatenate(picks, 1), wp[...])
     ready("eo")
     eo[...] = centre(eo[...])
-    arrived(first)
-
-    table[...] = dot(halo[...], ws[...]).astype(bf16)
-    for t in range(EDGES // EDGE_TILE):
-        rows = pl.ds(t * EDGE_TILE, EDGE_TILE)
-        inner = silu(
-            acc[rows, :] + dot(one_hot(edge_rows(t, es), NODES, TABLE // LANES), table[...])
-        )
-        outer = dot(inner, eo[...])
-        message[rows, :] = (outer * inverse_spread(outer)).astype(bf16)
-
     ready("ni", "no")
     no[...] = centre(no[...])
-
-    def node_update(latent, placing):
-        summed = dot(placing, message[...]).astype(bf16)
-        inner = silu(dot(jnp.concatenate([latent, summed], 1), ni[...]))
-        outer = dot(inner, no[...])
-        return (latent.astype(f32) + outer * inverse_spread(outer)).astype(bf16)
 
     def placing(nodes):
         blocks = [
@@ -250,7 +236,26 @@
         ]
         return jnp.concatenate(blocks, 1)
 
-    chosen_new[...] = node_update(chosen[...], placing(sent_rows))
+    into_sent[...] = placing(sent_rows)
+    arrived(first)
+
+    table[...] = dot(halo[...], ws[...]).astype(bf16)
+    for t in range(EDGES // EDGE_TILE):
+        rows = pl.ds(t * EDGE_TILE, EDGE_TILE)
+        inner = silu(
+            acc[rows, :] + dot(from_halo[rows, :], table[...])
+        )
+        outer = dot(inner, eo[...])
+        message[rows, :] = (outer * inverse_spread(outer)).astype(bf16)
+
+
+    def node_update(latent, placing):
+        summed = dot(placing, message[...]).astype(bf16)
+        inner = silu(dot(jnp.concatenate([latent, summed], 1), ni[...]))
+        outer = dot(inner, no[...])
+        return (latent.astype(f32) + outer * inverse_spread(outer)).astype(bf16)
+
+    chosen_new[...] = node_update(chosen[...], into_sent[...])
     second = exchange(chosen_new, halo_new, send_new_sem, recv_new_sem)
 
     for t in range(NODES // NODE_TILE):
@@ -266,7 +271,9 @@
 
     for t in range(DECODER // GRID_TILE):
         rows = pl.ds(t * GRID_TILE, GRID_TILE)
-        picks = [glat[rows, :], one_hot(grid_rows(t), 0, NODES // LANES)]
+        senders = grid_rows(t)
+        grid_from_halo[rows, :] = one_hot(senders, NODES, TABLE // LANES)
+        picks = [glat[rows, :], one_hot(senders, 0, NODES // LANES)]
         acc_grid[rows, :] = dot(jnp.concatenate(picks, 1), gwp[...])
     ready("go", "ow", "prior", "target", "cw", "aw")
     go[...] = centre(go[...])
@@ -278,7 +285,7 @@
     for t in range(DECODER // GRID_TILE):
         rows = pl.ds(t * GRID_TILE, GRID_TILE)
         inner = silu(
-            acc_grid[rows, :] + dot(one_hot(grid_rows(t), NODES, TABLE // LANES), table[...])
+            acc_grid[rows, :] + dot(grid_from_halo[rows, :], table[...])
         )
         outer = dot(inner, go[...])
         channels = lax.dot_general(
@@ -395,6 +402,9 @@
         vmem((SENT, WIDTH), bf16),
         vmem((TABLE, WIDTH), bf16),
         vmem((TABLE, WIDTH), bf16),
+        vmem((EDGES, TABLE), bf16),
+        vmem((SENT, EDGES), bf16),
+        vmem((DECODER, TABLE), bf16),
         vmem((EDGES, WIDTH), f32),
         vmem((DECODER, WIDTH), f32),
         vmem((EDGES // LANES, LANES), jnp.int32),
@@ -422,7 +432,7 @@
     ]
     return pl.pallas_call(
         kernel,
-        out_shape=jax.ShapeDtypeStruct((1, CHANNELS, POINTS), f32),
+        out_shape=pltpu.VMEM((1, CHANNELS, POINTS), f32),
         in_specs=[hbm] * 19,
         out_specs=pl.BlockSpec(memory_space=pltpu.VMEM),
         scratch_shapes=scratch,

time: 32.5 us -> 30.2 us (0.929)
  Pallas kernels: 29.9 us -> 28.6 us
  local copies, waits for them, and re-layouts: 1.78 us -> 0.86 us
    pallas_call x1, Pallas kernels: 29.9 us -> 28.6 us  [per_device(): pl.pallas_call(kernel, out_shape=pltpu.VMEM((1, CHANNELS, POINTS), f32),...]
    pallas_call x1, local copies, waits for them, and re-layouts: 1.78 us -> 0.86 us  [per_device(): pl.pallas_call(kernel, out_shape=pltpu.VMEM((1, CHANNELS, POINTS), f32),...]
where the time goes in v3:
time: 30.2 us; the launch traced here: 30.1 us
  Pallas kernels  28.6 us (95%)
  local copies, waits for them, and re-layouts  0.86 us (3%)
  between operations  0.66 us (2%)
    pallas_call x1, Pallas kernels, per_device(): pl.pallas_call(kernel, out_shape=pltpu.VMEM((1, CHANNELS, POINTS), f32),...  28.6 us
    pallas_call x1, local copies, waits for them, and re-layouts, per_device(): pl.pallas_call(kernel, out_shape=pltpu.VMEM((1, CHANNELS, POINTS), f32),...  0.86 us

profile of v3, /device:TPU:7, one launch (start us, length us, event | category | flops | bytes accessed | tf_op | source)
XLA Modules:
  0.0 30.1 jit_solution(4211802171919145314)
XLA Ops:
  0.7 28.6 %ensemble_layers.1 = f32[1,87,512]{2,1,0:T(8,128)S(1)} custom-call(bf16[1,512,512]{2,1,0:T(8,128)(2,1)} %lat_h.1, bf16[1024,512]{1,0:T(8,128)(2,1)} %elat_h.1, bf16[1536,512]{1,0:T(8,128)(2,1)} %glat_h.1, bf16[1536,512]{1,0:T(8,128)(2,1)} %ei_h.1, bf16[512,512]{1,0:T(8,128)(2,1)} %eo_h.1, bf16[1024,512]{1,0:T(8,128)(2,1)} %ni_h.1, bf16[512,512]{1,0:T(8,128)(2,1)} %no_h.1, ...), custom_call_target="tpu_custom_call" | custom-call | flops 8999999488 | bytes 9000000 | tf_op jit(solution)/shard_map/ensemble_layers/pallas_call | solution.py:433
  29.2 0.9 %copy.20 = f32[1,87,512]{2,0,1:T(1,128)} copy(f32[1,87,512]{2,1,0:T(8,128)S(1)} %ensemble_layers.1) | data formatting | bytes 356352 | tf_op jit(solution)/shard_map/ensemble_layers/pallas_call | solution.py:433

commit v4 on v3

--- a/solution.py
+++ b/solution.py
@@ -24,6 +24,7 @@
 CHANNELS = 87
 PADDED = 96
 MEMBERS = 8
+Z_ROW = 8
 PEERS = 3
 CHUNKS = 2
 CHUNK = POINTS // CHUNKS
@@ -51,8 +52,8 @@
 
 
 def silu(v):
-    half = 0.5 * v
-    return (half + half * jnp.tanh(half)).astype(bf16)
+    half = (0.5 * v).astype(bf16)
+    return half + half * jnp.tanh(half)
 
 
 def inverse_spread(centred):
@@ -72,8 +73,8 @@
     lat_h, elat_h, glat_h, ei_h, eo_h, ni_h, no_h, gi_h, go_h, ow_h, prior_h, target_h,
     cw_h, aw_h, sends_h, es_h, er_h, gs_h, count_h,
     out_ref,
-    lat, elat, glat, ws, wr, wp, eo, ni, no, gws, gwp, go, ow, prior, target, cw, aw, sends, es, er, gs, count,
-    chosen, halo, chosen_new, halo_new, table, from_halo, into_sent, grid_from_halo, acc, acc_grid, live, message, updated, readout,
+    lat, elat, glat, ws, wr, wp, eo, ni, no, gws, gwe, node_part, go, ow, prior, target, cw, aw, sends, es, er, gs, count,
+    chosen, halo, chosen_new, halo_new, table, from_halo, into_sent, grid_from_own, grid_from_halo, acc, acc_grid, live, message, updated, readout_weight, readout,
     diff, outgoing, incoming, beside, pairwise, partial, partial_in,
     load_sem, send_sem, recv_sem, send_new_sem, recv_new_sem, peer_sem, peer_in_sem, beside_sem, beside_in_sem,
     partial_sem, partial_in_sem,
@@ -88,28 +89,14 @@
     sibling = member + 1 - 2 * lax.rem(member, 2)
     peers = [lax.rem(member + 2 * k, MEMBERS) for k in range(1, PEERS + 1)]
 
-    barrier = pltpu.get_barrier_semaphore()
-
-    def greet(other, row):
-        pl.semaphore_signal(barrier, inc=1, device_id=(other, row), device_id_type=MESH)
-
-    @pl.when(has_above)
-    def _():
-        greet(member, above)
-
-    @pl.when(has_below)
-    def _():
-        greet(member, below)
-
-    for other in peers + [sibling]:
-        greet(other, band)
-
     loads = {}
 
     def load(name, source, target_ref):
-        copy = pltpu.make_async_copy(source, target_ref, load_sem.at[len(loads)])
-        copy.start()
-        loads[name] = copy
+        loads[name] = pltpu.make_async_copy(source, target_ref, load_sem.at[len(loads)])
+
+    def begin(*names):
+        for name in names:
+            loads[name].start()
 
     def ready(*names):
         for name in names:
@@ -124,6 +111,37 @@
     load("count", count_h, count)
     load("we", ei_h.at[pl.ds(2 * WIDTH, WIDTH)], wp.at[pl.ds(0, WIDTH)])
     load("elat", elat_h, elat)
+    load("eo", eo_h, eo)
+    load("ni", ni_h, ni)
+    load("no", no_h, no)
+    load("gws", gi_h.at[pl.ds(0, WIDTH)], gws)
+    load("gwe", gi_h.at[pl.ds(WIDTH, WIDTH)], gwe)
+    load("gs", gs_h, gs)
+    load("glat", glat_h, glat)
+    load("go", go_h, go)
+    load("ow", ow_h, ow)
+    load("prior", prior_h, prior)
+    load("target", target_h, target)
+    load("cw", cw_h, cw)
+    load("aw", aw_h, aw)
+    begin("sends", "lat")
+    barrier = pltpu.get_barrier_semaphore()
+
+    def greet(other, row):
+        pl.semaphore_signal(barrier, inc=1, device_id=(other, row), device_id_type=MESH)
+
+    @pl.when(has_above)
+    def _():
+        greet(member, above)
+
+    @pl.when(has_below)
+    def _():
+        greet(member, below)
+
+    for other in peers + [sibling]:
+        greet(other, band)
+
+    begin("ws", "wr", "es", "er", "count")
     ready("sends")
     up = spread(jnp.concatenate([sends[0:1, :], jnp.zeros((1, LANES - HALO), jnp.int32)], 1))
     down = spread(jnp.concatenate([sends[1:2, :], jnp.zeros((1, LANES - HALO), jnp.int32)], 1))
@@ -140,7 +158,71 @@
             rows[HALO:SENT, :] = jnp.zeros((HALO, WIDTH), bf16)
 
     ready("lat")
+    begin("we", "elat")
     chosen[...] = dot(one_hot(sent_rows, 0, NODES // LANES), lat[...]).astype(bf16)
+
+    def edge_rows(t, indices):
+        each = EDGE_TILE // LANES
+        return jnp.concatenate(
+            [spread(indices[pl.ds(t * each + i, 1), :]) for i in range(each)], 0
+        )
+
+    def placing(nodes):
+        blocks = [
+            jnp.where(nodes == live[i : i + 1, :], 1.0, 0.0).astype(bf16)
+            for i in range(EDGES // LANES)
+        ]
+        return jnp.concatenate(blocks, 1)
+
+    def grid_rows(t):
+        each = GRID_TILE // LANES
+        return jnp.concatenate([spread(gs[pl.ds(t * each + i, 1), :]) for i in range(each)], 0)
+
+    def edge_products():
+        ready("ws", "wr", "es", "er", "count")
+        wp[pl.ds(WIDTH, WIDTH), :] = dot(lat[...], ws[...]).astype(bf16)
+        wp[pl.ds(2 * WIDTH, WIDTH), :] = dot(lat[...], wr[...]).astype(bf16)
+        slots = (
+            lax.broadcasted_iota(jnp.int32, (EDGES // LANES, LANES), 0) * LANES
+            + lax.broadcasted_iota(jnp.int32, (EDGES // LANES, LANES), 1)
+        )
+        live[...] = jnp.where(slots < count[...], er[...], -1)
+        ready("we", "elat")
+        for t in range(EDGES // EDGE_TILE):
+            rows = pl.ds(t * EDGE_TILE, EDGE_TILE)
+            senders = edge_rows(t, es)
+            from_halo[rows, :] = one_hot(senders, NODES, TABLE // LANES)
+            picks = [
+                elat[rows, :],
+                one_hot(senders, 0, NODES // LANES),
+                one_hot(edge_rows(t, er), 0, NODES // LANES),
+            ]
+            acc[rows, :] = dot(jnp.concatenate(picks, 1), wp[...])
+        ready("eo")
+        eo[...] = centre(eo[...])
+        ready("ni", "no")
+        no[...] = centre(no[...])
+        into_sent[...] = placing(sent_rows)
+
+    def decoder_products():
+        ready("gwe", "gs", "glat")
+        for t in range(DECODER // GRID_TILE):
+            rows = pl.ds(t * GRID_TILE, GRID_TILE)
+            senders = grid_rows(t)
+            grid_from_own[rows, :] = one_hot(senders, 0, NODES // LANES)
+            grid_from_halo[rows, :] = one_hot(senders, NODES, TABLE // LANES)
+            acc_grid[rows, :] = dot(glat[rows, :], gwe[...])
+
+    def begin_rest():
+        begin("eo", "ni", "no", "gws", "gwe", "gs", "glat", "go", "ow", "prior", "target", "cw", "aw")
+
+    ahead = lax.rem(band, Z_ROW) == 0
+
+    @pl.when(ahead)
+    def _():
+        begin_rest()
+        edge_products()
+        decoder_products()
 
     pl.semaphore_wait(
         barrier, PEERS + 1 + has_above.astype(jnp.int32) + has_below.astype(jnp.int32)
@@ -156,18 +238,16 @@
             device_id_type=MESH,
         )
 
-    def exchange(source, into, send, recv):
-        copies = []
-        for i, (there, neighbour) in enumerate(((has_above, above), (has_below, below))):
-            part = pl.ds(i * HALO, HALO)
-            copy = remote(source.at[part], into.at[part], send.at[i], recv.at[i], member, neighbour)
-            copies.append(copy)
-
-            @pl.when(there)
-            def _():
-                copy.start()
-
-        return copies
+    def exchange(source, into, send, recv, i):
+        there, neighbour = ((has_above, above), (has_below, below))[i]
+        part = pl.ds(i * HALO, HALO)
+        copy = remote(source.at[part], into.at[part], send.at[i], recv.at[i], member, neighbour)
+
+        @pl.when(there)
+        def _():
+            copy.start()
+
+        return copy
 
     def arrived(copies):
         for copy, there in zip(copies, (has_below, has_above)):
@@ -183,60 +263,13 @@
             def _():
                 copy.wait_send()
 
-    first = exchange(chosen, halo, send_sem, recv_sem)
-
-    load("eo", eo_h, eo)
-    load("ni", ni_h, ni)
-    load("no", no_h, no)
-    load("gws", gi_h.at[pl.ds(0, WIDTH)], gws)
-    load("gwe", gi_h.at[pl.ds(WIDTH, WIDTH)], gwp.at[pl.ds(0, WIDTH)])
-    load("gs", gs_h, gs)
-    load("glat", glat_h, glat)
-    load("go", go_h, go)
-    load("ow", ow_h, ow)
-    load("prior", prior_h, prior)
-    load("target", target_h, target)
-    load("cw", cw_h, cw)
-    load("aw", aw_h, aw)
-    ready("ws", "wr", "es", "er", "count")
-    wp[pl.ds(WIDTH, WIDTH), :] = dot(lat[...], ws[...]).astype(bf16)
-    wp[pl.ds(2 * WIDTH, WIDTH), :] = dot(lat[...], wr[...]).astype(bf16)
-    slots = (
-        lax.broadcasted_iota(jnp.int32, (EDGES // LANES, LANES), 0) * LANES
-        + lax.broadcasted_iota(jnp.int32, (EDGES // LANES, LANES), 1)
-    )
-    live[...] = jnp.where(slots < count[...], er[...], -1)
-    ready("we", "elat")
-
-    def edge_rows(t, indices):
-        each = EDGE_TILE // LANES
-        return jnp.concatenate(
-            [spread(indices[pl.ds(t * each + i, 1), :]) for i in range(each)], 0
-        )
-
-    for t in range(EDGES // EDGE_TILE):
-        rows = pl.ds(t * EDGE_TILE, EDGE_TILE)
-        senders = edge_rows(t, es)
-        from_halo[rows, :] = one_hot(senders, NODES, TABLE // LANES)
-        picks = [
-            elat[rows, :],
-            one_hot(senders, 0, NODES // LANES),
-            one_hot(edge_rows(t, er), 0, NODES // LANES),
-        ]
-        acc[rows, :] = dot(jnp.concatenate(picks, 1), wp[...])
-    ready("eo")
-    eo[...] = centre(eo[...])
-    ready("ni", "no")
-    no[...] = centre(no[...])
-
-    def placing(nodes):
-        blocks = [
-            jnp.where(nodes == live[i : i + 1, :], 1.0, 0.0).astype(bf16)
-            for i in range(EDGES // LANES)
-        ]
-        return jnp.concatenate(blocks, 1)
-
-    into_sent[...] = placing(sent_rows)
+    first = [exchange(chosen, halo, send_sem, recv_sem, i) for i in range(2)]
+
+    @pl.when(jnp.logical_not(ahead))
+    def _():
+        begin_rest()
+        edge_products()
+
     arrived(first)
 
     table[...] = dot(halo[...], ws[...]).astype(bf16)
@@ -256,27 +289,28 @@
         return (latent.astype(f32) + outer * inverse_spread(outer)).astype(bf16)
 
     chosen_new[...] = node_update(chosen[...], into_sent[...])
-    second = exchange(chosen_new, halo_new, send_new_sem, recv_new_sem)
+    second = [exchange(chosen_new, halo_new, send_new_sem, recv_new_sem, 0)]
 
     for t in range(NODES // NODE_TILE):
         rows = pl.ds(t * NODE_TILE, NODE_TILE)
         nodes = lax.broadcasted_iota(jnp.int32, (NODE_TILE, LANES), 0) + t * NODE_TILE
         updated[rows, :] = node_update(lat[rows, :], placing(nodes))
-    ready("gws", "gwe", "gs", "glat")
-    gwp[pl.ds(WIDTH, WIDTH), :] = dot(updated[...], gws[...]).astype(bf16)
-
-    def grid_rows(t):
-        each = GRID_TILE // LANES
-        return jnp.concatenate([spread(gs[pl.ds(t * each + i, 1), :]) for i in range(each)], 0)
-
+        if t == 0:
+            second.append(exchange(chosen_new, halo_new, send_new_sem, recv_new_sem, 1))
+
+    @pl.when(jnp.logical_not(ahead))
+    def _():
+        decoder_products()
+
+    ready("gws")
+    node_part[...] = dot(updated[...], gws[...]).astype(bf16)
     for t in range(DECODER // GRID_TILE):
         rows = pl.ds(t * GRID_TILE, GRID_TILE)
-        senders = grid_rows(t)
-        grid_from_halo[rows, :] = one_hot(senders, NODES, TABLE // LANES)
-        picks = [glat[rows, :], one_hot(senders, 0, NODES // LANES)]
-        acc_grid[rows, :] = dot(jnp.concatenate(picks, 1), gwp[...])
+        acc_grid[rows, :] += dot(grid_from_own[rows, :], node_part[...])
     ready("go", "ow", "prior", "target", "cw", "aw")
     go[...] = centre(go[...])
+    readout_weight[...] = jnp.zeros_like(readout_weight)
+    readout_weight[:, 0:CHANNELS] = ow[...].astype(f32).T.astype(bf16)
     arrived(second)
 
     table[...] = dot(halo_new[...], gws[...]).astype(bf16)
@@ -288,10 +322,8 @@
             acc_grid[rows, :] + dot(grid_from_halo[rows, :], table[...])
         )
         outer = dot(inner, go[...])
-        channels = lax.dot_general(
-            outer.astype(bf16), ow[...], (((1,), (1,)), ((), ())), preferred_element_type=f32
-        )
-        readout[rows, 0:CHANNELS] = channels * inverse_spread(outer)
+        channels = dot(outer.astype(bf16), readout_weight[...])
+        readout[rows, :] = channels * inverse_spread(outer)
         points = pl.ds(t * LANES, LANES)
         output = (
             readout[pl.ds(t * GRID_TILE, LANES, 3), :]
@@ -317,8 +349,12 @@
                     beside_in_sem.at[chunk], sibling, band,
                 )
             )
-            for copy in to_peers[-1] + to_sibling[-1:]:
-                copy.start()
+
+            @pl.when(band >= 0)
+            def _():
+                for copy in to_peers[-1] + to_sibling[-1:]:
+                    copy.start()
+
 
     gains = spread(
         jnp.concatenate([cw[...], jnp.zeros((1, LANES - CHANNELS), f32)], 1)
@@ -385,7 +421,8 @@
         vmem((2 * WIDTH, WIDTH), bf16),
         square,
         square,
-        vmem((2 * WIDTH, WIDTH), bf16),
+        square,
+        square,
         square,
         vmem((CHANNELS, WIDTH), bf16),
         vmem((CHANNELS, POINTS), f32),
@@ -404,12 +441,14 @@
         vmem((TABLE, WIDTH), bf16),
         vmem((EDGES, TABLE), bf16),
         vmem((SENT, EDGES), bf16),
+        vmem((DECODER, NODES), bf16),
         vmem((DECODER, TABLE), bf16),
         vmem((EDGES, WIDTH), f32),
         vmem((DECODER, WIDTH), f32),
         vmem((EDGES // LANES, LANES), jnp.int32),
         vmem((EDGES, WIDTH), bf16),
         vmem((NODES, WIDTH), bf16),
+        vmem((WIDTH, LANES), bf16),
         vmem((DECODER, LANES), f32),
         vmem((PADDED, POINTS), f32),
         vmem((CHUNKS, PADDED, CHUNK), bf16),

time: 30.2 us -> 29.6 us (0.980)
  Pallas kernels: 28.6 us -> 28 us
    pallas_call x1, Pallas kernels: 28.6 us -> 28 us  [per_device(): pl.pallas_call(kernel, out_shape=pltpu.VMEM((1, CHANNELS, POINTS), f32),...]
where the time goes in v4:
time: 29.6 us; the launch traced here: 29.5 us
  Pallas kernels  28 us (95%)
  local copies, waits for them, and re-layouts  0.86 us (3%)
  between operations  0.66 us (2%)
    pallas_call x1, Pallas kernels, per_device(): pl.pallas_call(kernel, out_shape=pltpu.VMEM((1, CHANNELS, POINTS), f32),...  28 us
    pallas_call x1, local copies, waits for them, and re-layouts, per_device(): pl.pallas_call(kernel, out_shape=pltpu.VMEM((1, CHANNELS, POINTS), f32),...  0.86 us

profile of v4, /device:TPU:7, one launch (start us, length us, event | category | flops | bytes accessed | tf_op | source)
XLA Modules:
  0.0 29.5 jit_solution(16469068864949868494)
XLA Ops:
  0.7 28.0 %ensemble_layers.1 = f32[1,87,512]{2,1,0:T(8,128)S(1)} custom-call(bf16[1,512,512]{2,1,0:T(8,128)(2,1)} %lat_h.1, bf16[1024,512]{1,0:T(8,128)(2,1)} %elat_h.1, bf16[1536,512]{1,0:T(8,128)(2,1)} %glat_h.1, bf16[1536,512]{1,0:T(8,128)(2,1)} %ei_h.1, bf16[512,512]{1,0:T(8,128)(2,1)} %eo_h.1, bf16[1024,512]{1,0:T(8,128)(2,1)} %ni_h.1, bf16[512,512]{1,0:T(8,128)(2,1)} %no_h.1, ...), custom_call_target="tpu_custom_call" | custom-call | flops 8999999488 | bytes 9000000 | tf_op jit(solution)/shard_map/ensemble_layers/pallas_call | solution.py:472
  28.7 0.9 %copy.20 = f32[1,87,512]{2,0,1:T(1,128)} copy(f32[1,87,512]{2,1,0:T(8,128)S(1)} %ensemble_layers.1) | data formatting | bytes 356352 | tf_op jit(solution)/shard_map/ensemble_layers/pallas_call | solution.py:472

commit v5 on v4

--- a/solution.py
+++ b/solution.py
@@ -189,6 +189,11 @@
         live[...] = jnp.where(slots < count[...], er[...], -1)
         ready("we", "elat")
         for t in range(EDGES // EDGE_TILE):
+            if t == EDGES // EDGE_TILE - 1:
+                ready("eo", "ni", "no")
+                into_sent[...] = placing(sent_rows)
+                eo[...] = centre(eo[...])
+                no[...] = centre(no[...])
             rows = pl.ds(t * EDGE_TILE, EDGE_TILE)
             senders = edge_rows(t, es)
             from_halo[rows, :] = one_hot(senders, NODES, TABLE // LANES)
@@ -198,11 +203,6 @@
                 one_hot(edge_rows(t, er), 0, NODES // LANES),
             ]
             acc[rows, :] = dot(jnp.concatenate(picks, 1), wp[...])
-        ready("eo")
-        eo[...] = centre(eo[...])
-        ready("ni", "no")
-        no[...] = centre(no[...])
-        into_sent[...] = placing(sent_rows)
 
     def decoder_products():
         ready("gwe", "gs", "glat")
@@ -303,14 +303,14 @@
         decoder_products()
 
     ready("gws")
+    ready("go", "ow", "prior", "target", "cw", "aw")
+    go[...] = centre(go[...])
+    readout_weight[...] = jnp.zeros_like(readout_weight)
+    readout_weight[:, 0:CHANNELS] = ow[...].astype(f32).T.astype(bf16)
     node_part[...] = dot(updated[...], gws[...]).astype(bf16)
     for t in range(DECODER // GRID_TILE):
         rows = pl.ds(t * GRID_TILE, GRID_TILE)
         acc_grid[rows, :] += dot(grid_from_own[rows, :], node_part[...])
-    ready("go", "ow", "prior", "target", "cw", "aw")
-    go[...] = centre(go[...])
-    readout_weight[...] = jnp.zeros_like(readout_weight)
-    readout_weight[:, 0:CHANNELS] = ow[...].astype(f32).T.astype(bf16)
     arrived(second)
 
     table[...] = dot(halo_new[...], gws[...]).astype(bf16)

time: 29.6 us -> 29.6 us (level)
  no operation moved by 1% of the time
where the time goes in v5:
time: 29.6 us; the launch traced here: 29.5 us
  Pallas kernels  28 us (95%)
  local copies, waits for them, and re-layouts  0.86 us (3%)
  between operations  0.66 us (2%)
    pallas_call x1, Pallas kernels, per_device(): pl.pallas_call(kernel, out_shape=pltpu.VMEM((1, CHANNELS, POINTS), f32),...  28 us
    pallas_call x1, local copies, waits for them, and re-layouts, per_device(): pl.pallas_call(kernel, out_shape=pltpu.VMEM((1, CHANNELS, POINTS), f32),...  0.86 us

profile of v5, /device:TPU:7, one launch (start us, length us, event | category | flops | bytes accessed | tf_op | source)
XLA Modules:
  0.0 29.5 jit_solution(16693310410356122175)
XLA Ops:
  0.7 28.0 %ensemble_layers.1 = f32[1,87,512]{2,1,0:T(8,128)S(1)} custom-call(bf16[1,512,512]{2,1,0:T(8,128)(2,1)} %lat_h.1, bf16[1024,512]{1,0:T(8,128)(2,1)} %elat_h.1, bf16[1536,512]{1,0:T(8,128)(2,1)} %glat_h.1, bf16[1536,512]{1,0:T(8,128)(2,1)} %ei_h.1, bf16[512,512]{1,0:T(8,128)(2,1)} %eo_h.1, bf16[1024,512]{1,0:T(8,128)(2,1)} %ni_h.1, bf16[512,512]{1,0:T(8,128)(2,1)} %no_h.1, ...), custom_call_target="tpu_custom_call" | custom-call | flops 8999999488 | bytes 9000000 | tf_op jit(solution)/shard_map/ensemble_layers/pallas_call | solution.py:472
  28.7 0.9 %copy.20 = f32[1,87,512]{2,0,1:T(1,128)} copy(f32[1,87,512]{2,1,0:T(8,128)S(1)} %ensemble_layers.1) | data formatting | bytes 356352 | tf_op jit(solution)/shard_map/ensemble_layers/pallas_call | solution.py:472

commit v6 on v5

--- a/solution.py
+++ b/solution.py
@@ -30,7 +30,7 @@
 CHUNK = POINTS // CHUNKS
 EDGE_TILE = 512
 GRID_TILE = 384
-NODE_TILE = 256
+NODE_TILE = 512
 
 
 def dot(a, b):
@@ -289,14 +289,12 @@
         return (latent.astype(f32) + outer * inverse_spread(outer)).astype(bf16)
 
     chosen_new[...] = node_update(chosen[...], into_sent[...])
-    second = [exchange(chosen_new, halo_new, send_new_sem, recv_new_sem, 0)]
+    second = [exchange(chosen_new, halo_new, send_new_sem, recv_new_sem, i) for i in range(2)]
 
     for t in range(NODES // NODE_TILE):
         rows = pl.ds(t * NODE_TILE, NODE_TILE)
         nodes = lax.broadcasted_iota(jnp.int32, (NODE_TILE, LANES), 0) + t * NODE_TILE
         updated[rows, :] = node_update(lat[rows, :], placing(nodes))
-        if t == 0:
-            second.append(exchange(chosen_new, halo_new, send_new_sem, recv_new_sem, 1))
 
     @pl.when(jnp.logical_not(ahead))
     def _():

time: 29.6 us -> 29.7 us (level)
  no operation moved by 1% of the time
where the time goes in v6:
time: 29.7 us; the launch traced here: 29.5 us
  Pallas kernels  28 us (94%)
  local copies, waits for them, and re-layouts  0.86 us (3%)
  between operations  0.66 us (2%)
    pallas_call x1, Pallas kernels, per_device(): pl.pallas_call(kernel, out_shape=pltpu.VMEM((1, CHANNELS, POINTS), f32),...  28 us
    pallas_call x1, local copies, waits for them, and re-layouts, per_device(): pl.pallas_call(kernel, out_shape=pltpu.VMEM((1, CHANNELS, POINTS), f32),...  0.86 us

profile of v6, /device:TPU:7, one launch (start us, length us, event | category | flops | bytes accessed | tf_op | source)
XLA Modules:
  0.0 29.5 jit_solution(5815785517002279608)
XLA Ops:
  0.7 28.0 %ensemble_layers.1 = f32[1,87,512]{2,1,0:T(8,128)S(1)} custom-call(bf16[1,512,512]{2,1,0:T(8,128)(2,1)} %lat_h.1, bf16[1024,512]{1,0:T(8,128)(2,1)} %elat_h.1, bf16[1536,512]{1,0:T(8,128)(2,1)} %glat_h.1, bf16[1536,512]{1,0:T(8,128)(2,1)} %ei_h.1, bf16[512,512]{1,0:T(8,128)(2,1)} %eo_h.1, bf16[1024,512]{1,0:T(8,128)(2,1)} %ni_h.1, bf16[512,512]{1,0:T(8,128)(2,1)} %no_h.1, ...), custom_call_target="tpu_custom_call" | custom-call | flops 8999999488 | bytes 9000000 | tf_op jit(solution)/shard_map/ensemble_layers/pallas_call | solution.py:470
  28.7 0.9 %copy.20 = f32[1,87,512]{2,0,1:T(1,128)} copy(f32[1,87,512]{2,1,0:T(8,128)S(1)} %ensemble_layers.1) | data formatting | bytes 356352 | tf_op jit(solution)/shard_map/ensemble_layers/pallas_call | solution.py:470
